TPU v7x, 512 devices: a whole 4x8x8 slice. The times are simulated.
512 devices in a mesh: dp: 16 (over y_hi, x), tp: 32 (over z, y_lo, core).
Axes of the slice: x: 4, y: 8 (y_hi: 4, y_lo: 2; y = y_hi * 2 + y_lo), z: 8, core: 2. Of those that a mesh axis runs over, the one named last changes fastest.
Arguments:
- queries: bfloat16 [16, 32, 2, 8192], P('dp', 'tp'), may hold values from -124 to 124
- residual: bfloat16 [16, 32, 2, 8192], P('dp', 'tp'), may hold values from -40 to 40
- new_entries: bfloat16 [16, 32, 2, 2048], P('dp', 'tp'), may hold values from -6 to 6
- page_pool: bfloat16 [16, 32, 32, 16, 2048], P('dp', 'tp'), may hold values from -5.6 to 5.6
- page_table: int32 [16, 32, 2, 16], P('dp', 'tp'), may hold values from 0 to 31, as said below
- cache_lengths: int32 [16, 32, 2], P('dp', 'tp'), may hold values from 1 to 256
- migration: int32 [32, 3, 3], P('tp'), may hold values from 0 to 15, as said below
- norm_gain: bfloat16 [8192], replicated, may hold values from 0.5 to 1.5
- gate_weight: bfloat16 [8192, 16384], P('dp', 'tp'), may hold values from -0.0625 to 0.0625
- up_weight: bfloat16 [8192, 16384], P('dp', 'tp'), may hold values from -0.0625 to 0.0625
- down_weight: bfloat16 [16384, 8192], P('tp', 'dp'), may hold values from -0.046875 to 0.046875
Outputs:
- layer_out: bfloat16 [16, 32, 2, 8192], P('dp', 'tp')
Inputs may be any that keep to these rules, and one draw needn't show every extreme that they name: `page_table`: each device's page tables name each of its 32 pool pages once. `migration`: for each tp index the 3 entries name one slot and 3 distinct source ranks; each entry's destination is the next entry's source, the last entry's destination the first entry's source.
All inputs are finite; a program needn't handle non-finite values.
Results may differ from a plain program's by a relative error of at most 0.014.
Values may be sent and summed in bfloat16 or wider, within the bound.
A program may use at most 64 MiB of HBM per device.

v0:
```python
import math

import jax
import jax.numpy as jnp
from jax import lax
from jax.sharding import PartitionSpec as P

HQ = 64
KVH = 8
HD = 128


epsilon = 1e-05


def spread(value, axis, source):
    kept = jnp.where(lax.axis_index(axis) == source, value, 0).astype(value.dtype)
    return lax.psum(kept, axis)


def attend_rows(head_rows, fresh_rows, caches, lengths):
    row_count = head_rows.shape[0]
    positions = caches.shape[1]
    groups = HQ // KVH
    factor = 1.0 / math.sqrt(HD)
    head_query = head_rows.reshape(row_count, KVH, groups, HD)
    key_rows = caches[:, :, : KVH * HD].reshape(row_count, positions, KVH, HD)
    value_rows = caches[:, :, KVH * HD :].reshape(row_count, positions, KVH, HD)
    own_key = fresh_rows[:, : KVH * HD].reshape(row_count, KVH, HD)
    own_value = fresh_rows[:, KVH * HD :].reshape(row_count, KVH, HD)
    scores = (
        jnp.einsum("nkgd,nlkd->nkgl", head_query, key_rows, preferred_element_type=jnp.float32)
        * factor
    )
    visible = jnp.arange(positions)[None, :] < lengths[:, None]
    scores = jnp.where(visible[:, None, None, :], scores, -jnp.inf)
    own_score = (
        jnp.einsum("nkgd,nkd->nkg", head_query, own_key, preferred_element_type=jnp.float32)
        * factor
    )
    highest = jnp.maximum(jnp.max(scores, axis=-1), own_score)
    exponent = jnp.exp(scores - highest[..., None])
    own_exponent = jnp.exp(own_score - highest)
    denominator = jnp.sum(exponent, axis=-1) + own_exponent
    weights = (exponent / denominator[..., None]).astype(jnp.bfloat16)
    own_weight = (own_exponent / denominator).astype(jnp.bfloat16)
    attended = jnp.einsum(
        "nkgl,nlkd->nkgd", weights, value_rows, preferred_element_type=jnp.float32
    )
    attended = (
        attended
        + own_weight.astype(jnp.float32)[..., None] * own_value.astype(jnp.float32)[:, :, None, :]
    )
    return attended.reshape(row_count, HQ * HD)


def on_device(
    queries,
    residual,
    new_entries,
    page_pool,
    page_table,
    cache_lengths,
    migration,
    norm_gain,
    gate_weight,
    up_weight,
    down_weight,
):
    head_rows = queries[0, 0]
    fresh_rows = new_entries[0, 0]
    pool_pages = page_pool[0, 0]
    tables = page_table[0, 0]
    own_lengths = cache_lengths[0, 0]
    entries = migration[0]
    slot_count = head_rows.shape[0]
    positions = tables.shape[1] * pool_pages.shape[1]
    own_caches = pool_pages[tables].reshape(slot_count, positions, pool_pages.shape[2])
    my_rank = lax.axis_index("dp")
    slot_place = jnp.arange(slot_count, dtype=jnp.int32)
    caches = own_caches
    lengths = own_lengths
    for entry_index in range(entries.shape[0]):
        slot_id = entries[entry_index, 0]
        source = entries[entry_index, 1]
        target = entries[entry_index, 2]
        outgoing = lax.dynamic_index_in_dim(own_caches, slot_id, 0, keepdims=False)
        sent_length = lax.dynamic_index_in_dim(own_lengths, slot_id, 0, keepdims=True).astype(
            jnp.bfloat16
        )
        arrived, arrived_length = (
            spread(outgoing, "dp", source),
            spread(sent_length, "dp", source),
        )
        taking = my_rank == target
        current = lax.dynamic_index_in_dim(caches, slot_id, 0, keepdims=False)
        caches = lax.dynamic_update_index_in_dim(
            caches, jnp.where(taking, arrived, current), slot_id, 0
        )
        lengths = jnp.where(
            taking & (slot_place == slot_id), arrived_length.astype(jnp.int32)[0], lengths
        )
    attended = attend_rows(head_rows, fresh_rows, caches, lengths)
    stream = residual[0, 0].astype(jnp.float32) + attended
    normed = (
        stream
        * lax.rsqrt(jnp.mean(stream * stream, axis=-1, keepdims=True) + epsilon)
        * norm_gain.astype(jnp.float32)
    ).astype(jnp.bfloat16)
    pieces = lax.all_to_all(normed, "dp", split_axis=1, concat_axis=0, tiled=True)
    gathered = lax.all_gather(pieces, "tp", axis=0, tiled=True)
    local_units = gate_weight.shape[1]
    summed = lax.psum_scatter(
        jnp.concatenate(
            [
                jnp.dot(gathered, gate_weight, preferred_element_type=jnp.float32),
                jnp.dot(gathered, up_weight, preferred_element_type=jnp.float32),
            ],
            axis=1,
        ).astype(jnp.bfloat16),
        "dp",
        scatter_dimension=0,
        tiled=True,
    ).astype(jnp.float32)
    hidden = (jax.nn.silu(summed[:, :local_units]) * summed[:, local_units:]).astype(jnp.bfloat16)
    partial_value = jnp.dot(
        lax.all_gather(hidden, "dp", axis=0, tiled=True),
        down_weight,
        preferred_element_type=jnp.float32,
    )
    ffn = lax.psum_scatter(
        partial_value.astype(jnp.bfloat16), "tp", scatter_dimension=0, tiled=True
    )
    returned_rows = lax.all_to_all(ffn, "dp", split_axis=0, concat_axis=1, tiled=True)
    layer_out = (stream + returned_rows.astype(jnp.float32)).astype(jnp.bfloat16)
    return layer_out.reshape(1, 1, slot_count, layer_out.shape[1])


def solution(mesh):
    return jax.shard_map(
        on_device,
        mesh=mesh,
        in_specs=(
            P("dp", "tp", None, None),
            P("dp", "tp", None, None),
            P("dp", "tp", None, None),
            P("dp", "tp", None, None, None),
            P("dp", "tp", None, None),
            P("dp", "tp", None),
            P("tp", None, None),
            P(),
            P("dp", "tp"),
            P("dp", "tp"),
            P("tp", "dp"),
        ),
        out_specs=P("dp", "tp", None, None),
        check_vma=False,
    )
```

profile of v0, /device:TPU:1, one launch (start us, length us, event | category | flops | bytes accessed | tf_op | source)
XLA Modules:
  0.0 624.4 jit_solution(5314091950665332835)
XLA Ops:
  6.5 0.8 copy.73
  7.4 0.7 fusion.19
  13.1 0.7 compare_select_fusion
  16.3 2.0 gather_fusion
  18.3 2.5 bitcast_select_fusion.3
  20.8 1.6 constant_dynamic-slice_fusion.2
  23.0 0.7 constant_dynamic-slice_fusion.5
  25.6 43.6 %all-reduce = (bf16[]{:T(256)}, bf16[]{:T(256)}, bf16[]{:T(256)}) all-reduce(bf16[]{:T(256)} %bitcast.17, bf16[]{:T(256)} %bitcast.11, bf16[]{:T(256)} %bitcast.5), channel_id=1, replica_groups=mesh['dp'=16,'tp'=32] {'dp'}, use_global_device_ids=true, to_apply=%region_2.3 | all-reduce | flops 3 | bytes 12 | tf_op jit(solution)/shard_map/psum | solution.py:18
  73.6 1.9 and_select_fusion.2
  75.7 150.6 %all-reduce.4.cloned.1.call-done = (bf16[256,2048]{1,0:T(8,128)(2,1)}, bf16[256,2048]{1,0:T(8,128)(2,1)}, bf16[256,2048]{1,0:T(8,128)(2,1)}) async-done(((bf16[256,2048]{1,0:T(8,128)(2,1)}, bf16[256,2048]{1,0:T(8,128)(2,1)}, bf16[256,2048]{1,0:T(8,128)(2,1)}), (bf16[256,2048]{1,0:T(8,128)(2,1)}, bf16[256,2048]{1,0:T(8,128)(2,1)}, bf16[256,2048]{1,0:T(8,128)(2,1)})) %all-reduce.4.cloned.1.call-update) | async-done | bytes 3145744 | tf_op jit(solution)/shard_map/psum | solution.py:18
  226.4 1.4 bitcast_dynamic-update-slice_fusion.2
  227.8 1.4 constant_dynamic-slice_fusion.1
  230.2 0.7 copy-done.3
  231.3 1.5 fusion.18
  232.8 1.5 copy.40
  235.4 1.5 copy.42
  236.9 1.8 fusion.5
  239.5 12.3 %all_to_all.29 = bf16[2,16,512]{2,0,1:T(2,128)(2,1)S(1)} all-to-all(bf16[2,16,512]{2,0,1:T(2,128)(2,1)S(1)} %copy.44), channel_id=1, replica_groups=mesh['dp'=16,'tp'=32] {'dp'}, dimensions={1} | all-to-all | bytes 65536 | tf_op jit(solution)/shard_map/all_to_all | solution.py:110
  252.4 69.0 %all-gather.3.cloned.1.call-done = bf16[1024,512]{1,0:T(8,128)(2,1)} async-done(((bf16[32,512]{1,0:T(8,128)(2,1)}), bf16[1024,512]{1,0:T(8,128)(2,1)}) %all-gather.3.cloned.1.call-update) | async-done | bytes 1048592 | tf_op jit(solution)/shard_map/all_gather | solution.py:111
  321.4 2.2 convolution_convert_fusion.1
  323.6 0.8 convolution_convert_fusion.2
  324.4 1.5 pad_maximum_fusion
  325.9 4.0 copy.51
  329.9 90.3 %reduce-scatter.7.cloned.1.call-done = bf16[64,1024]{1,0:T(8,128)(2,1)} async-done(((bf16[1024,1024]{1,0:T(8,128)(2,1)}), bf16[64,1024]{1,0:T(8,128)(2,1)}) %reduce-scatter.7.cloned.1.call-update) | async-done | bytes 131088 | tf_op jit(solution)/shard_map/reduce_scatter | solution.py:113
  420.2 0.9 convert_element_type.116
  421.1 0.7 fusion.2
  421.9 59.0 %all-gather.5.cloned.1.call-done = bf16[1024,512]{1,0:T(8,128)(2,1)} async-done(((bf16[64,512]{1,0:T(8,128)(2,1)}), bf16[1024,512]{1,0:T(8,128)(2,1)}) %all-gather.5.cloned.1.call-update) | async-done | bytes 1048592 | tf_op jit(solution)/shard_map/all_gather | solution.py:127
  480.9 2.9 convolution_convert_fusion
  483.8 115.1 %reduce-scatter.5.cloned.1.call-done = bf16[32,512]{1,0:T(8,128)(2,1)} async-done(((bf16[1024,512]{1,0:T(8,128)(2,1)}), bf16[32,512]{1,0:T(8,128)(2,1)}) %reduce-scatter.5.cloned.1.call-update) | async-done | bytes 32784 | tf_op jit(solution)/shard_map/reduce_scatter | solution.py:131
  598.9 1.4 all_to_all.25
  600.3 8.0 %all-to-all-start.1 = ((bf16[16,2,512]{2,1,0:T(2,128)(2,1)}), bf16[16,2,512]{2,1,0:T(2,128)(2,1)S(1)}, u32[]{:S(2)}, u32[]{:S(2)}) async-start(bf16[16,2,512]{2,1,0:T(2,128)(2,1)} %all_to_all.25), calls=%async_computation.2 | async-start | bytes 65536 | tf_op jit(solution)/shard_map/all_to_all | solution.py:134
  608.4 8.8 %all-to-all-done.1 = bf16[16,2,512]{2,1,0:T(2,128)(2,1)S(1)} async-done(((bf16[16,2,512]{2,1,0:T(2,128)(2,1)}), bf16[16,2,512]{2,1,0:T(2,128)(2,1)S(1)}, u32[]{:S(2)}, u32[]{:S(2)}) %all-to-all-start.1) | async-done | bytes 32800 | tf_op jit(solution)/shard_map/all_to_all | solution.py:134
  (60 shorter events, 6.4 us)
Async XLA Ops:
  6.5 9.8 %copy-start = (bf16[1,1,32,16,2048]{4,3,2,1,0:T(8,128)(2,1)S(1)}, bf16[1,1,32,16,2048]{4,3,2,1,0:T(8,128)(2,1)}, u32[]{:S(2)}) copy-start(bf16[1,1,32,16,2048]{4,3,2,1,0:T(8,128)(2,1)} %param.14) | copy-start | bytes 6291460
  6.5 219.8 %all-reduce.4.cloned.1.call-start = ((), (), s32[]{:S(2)}) async-start(), calls=%async_computation.8 | async-start | bytes 6291456 | tf_op jit(solution)/shard_map/psum | solution.py:18
  18.3 2.5 copy-start.1
  22.4 0.7 copy-start.9
  22.4 50.6 %copy-start.8 = (bf16[1,1,2,2048]{3,2,1,0:T(2,128)(2,1)S(1)}, bf16[1,1,2,2048]{3,2,1,0:T(2,128)(2,1)}, u32[]{:S(2)}) copy-start(bf16[1,1,2,2048]{3,2,1,0:T(2,128)(2,1)} %param.13) | copy-start | bytes 24580
  22.4 51.2 %copy-start.5 = (bf16[1,1,2,8192]{3,2,1,0:T(2,128)(2,1)S(1)}, bf16[1,1,2,8192]{3,2,1,0:T(2,128)(2,1)}, u32[]{:S(2)}) copy-start(bf16[1,1,2,8192]{3,2,1,0:T(2,128)(2,1)} %param.12) | copy-start | bytes 98308
  22.4 51.2 %copy-start.7 = (bf16[8192]{0:T(1024)(128)(2,1)S(1)}, bf16[8192]{0:T(1024)(128)(2,1)}, u32[]{:S(2)}) copy-start(bf16[8192]{0:T(1024)(128)(2,1)} %param.18) | copy-start | bytes 49156
  22.4 53.2 %copy-start.6 = (bf16[1,1,2,8192]{3,2,1,0:T(2,128)(2,1)S(1)}, bf16[1,1,2,8192]{3,2,1,0:T(2,128)(2,1)}, u32[]{:S(2)}) copy-start(bf16[1,1,2,8192]{3,2,1,0:T(2,128)(2,1)} %param.11) | copy-start | bytes 98308
  22.4 299.0 %all-gather.3.cloned.1.call-start = ((), (), s32[]{:S(2)}) async-start(), calls=%async_computation.4 | async-start | bytes 1081344 | tf_op jit(solution)/shard_map/all_gather | solution.py:111
  226.4 2.8 copy-start.4
  227.8 1.9 copy-start.2
  229.7 1.2 copy-start.3
  238.6 84.9 %copy-start.11 = (bf16[512,512]{1,0:T(8,128)(2,1)S(1)}, bf16[512,512]{1,0:T(8,128)(2,1)}, u32[]{:S(2)}) copy-start(bf16[512,512]{1,0:T(8,128)(2,1)} %param.19) | copy-start | bytes 1572868
  252.4 167.8 %reduce-scatter.7.cloned.1.call-start = ((), (), s32[]{:S(2)}) async-start(), calls=%async_computation.7 | async-start | bytes 2228224 | tf_op jit(solution)/shard_map/reduce_scatter | solution.py:113
  321.4 2.2 copy-start.10
  329.8 151.1 %copy-start.12 = (bf16[512,512]{1,0:T(8,128)(2,1)S(1)}, bf16[512,512]{1,0:T(8,128)(2,1)}, u32[]{:S(2)}) copy-start(bf16[512,512]{1,0:T(8,128)(2,1)} %param.21) | copy-start | bytes 1572868
  329.9 151.0 %all-gather.5.cloned.1.call-start = ((), (), s32[]{:S(2)}) async-start(), calls=%async_computation.5 | async-start | bytes 1114112 | tf_op jit(solution)/shard_map/all_gather | solution.py:127
  421.8 177.1 %reduce-scatter.5.cloned.1.call-start = ((), (), s32[]{:S(2)}) async-start(), calls=%async_computation.6 | async-start | bytes 1081344 | tf_op jit(solution)/shard_map/reduce_scatter | solution.py:131
  600.3 16.9 %all-to-all-start.1 = ((bf16[16,2,512]{2,1,0:T(2,128)(2,1)}), bf16[16,2,512]{2,1,0:T(2,128)(2,1)S(1)}, u32[]{:S(2)}, u32[]{:S(2)}) async-start(bf16[16,2,512]{2,1,0:T(2,128)(2,1)} %all_to_all.25), calls=%async_computation.2 | async-start | bytes 65536 | tf_op jit(solution)/shard_map/all_to_all | solution.py:134
Sparse Core Ops, SparseCore 0:
  22.5 203.7 all-reduce.3
  252.5 68.8 all-gather.2
  330.0 90.1 reduce-scatter.6
  423.5 57.3 all-gather.4
  483.9 114.9 reduce-scatter.4
where the time goes:
time: 629 us; the launch traced here: 624 us
  waiting for transfers between devices  493 us (78%)
  blocking collectives  55.9 us (9%)
  between operations  26.5 us (4%)
  local copies, waits for them, and re-layouts  18.7 us (3%)
  other arithmetic  14.2 us (2%)
  starting transfers between devices  8.19 us (1%)
  matrix products  8.08 us (1%)
    psum x1, waiting for transfers between devices, spread(): return lax.psum(kept, axis)  151 us
    reduce_scatter x1, waiting for transfers between devices, on_device(): lax.psum_scatter(partial_value.astype(jnp.bfloat16), 'tp', scatter_dimens...  115 us
    reduce_scatter x1, waiting for transfers between devices, on_device(): lax.psum_scatter(jnp.concatenate([jnp.dot(gathered, gate_weight, preferre...  90.3 us
    all_gather x1, waiting for transfers between devices, on_device(): gathered = lax.all_gather(pieces, 'tp', axis=0, tiled=True)  69 us
    all_gather x1, waiting for transfers between devices, on_device(): lax.all_gather(hidden, 'dp', axis=0, tiled=True)  59 us
    psum x1, blocking collectives, spread(): return lax.psum(kept, axis)  43.6 us
  transfers between devices with their start and end apart: 6, of which 6 were waited for; matrix products, arithmetic and copies ran while one was open for 1% of the time, Pallas kernels for 0%

commit v1 on v0

v1 whole, which is shorter than its diff:
```python
import functools
import math

import jax
import jax.numpy as jnp
from jax import lax
from jax.experimental import pallas as pl
from jax.experimental.pallas import tpu as pltpu
from jax.sharding import PartitionSpec as P

HD = 128
KVH = 8
NX, NH, NZ = 4, 4, 8
DP = NX * NH
MIG = 3
CHUNKS = ((0, 1), (-3, 4), (-2, 3), (-1, 2))
EPSILON = 1e-05
BF = jnp.bfloat16
F32 = jnp.float32


def kernel(
    plan, own, bias, gain, pool, gate_w, up_w, down_w, out,
    pool_v, gate_v, up_v, down_v,
    route_a, b_send, route_b, c_send, spread_c, tiles, x_all,
    gate_p, up_p, m1g, m1u, m2g, m2u, s3g, s3u, m3g, m3u,
    h_send, h_recv, hid, part, part_in, z_send, z_recv, l_send, l_recv,
    e_send, e_recv,
    load_sem, a_s, a_r, b_s, b_r, c_s, c_r, e_s, e_r,
    xl_s, xl_r, xz_s, xz_r, xc_s, xc_r,
    xp_s, xp_r, hp_s, hp_r, hg_s, hg_r, xg_s, xg_r,
    oc_s, oc_r, oz_s, oz_r, ol_s, ol_r,
):
    dp, tp = lax.axis_index("dp"), lax.axis_index("tp")
    h, x = lax.div(dp, NX), lax.rem(dp, NX)
    z, low = lax.div(tp, 4), lax.rem(tp, 4)
    l, c = lax.div(low, 2), lax.rem(low, 2)
    other_l, other_c = 1 - l, 1 - c
    xr, xo, xl = lax.rem(x + 1, NX), lax.rem(x + 2, NX), lax.rem(x + 3, NX)

    def at_dp(rank):
        return (rank, tp)

    def at_x(place):
        return (h * NX + place, tp)

    def at_h(place):
        return (place * NX + x, tp)

    def at_tp(zz, ll, cc):
        return (dp, zz * 4 + ll * 2 + cc)

    def z_at(offset):
        return lax.rem(z + (offset + NZ), NZ)

    sent = []

    def send(src, dst, send_sem, recv_sem, device):
        copy = pltpu.make_async_remote_copy(
            src_ref=src, dst_ref=dst, send_sem=send_sem, recv_sem=recv_sem,
            device_id=device, device_id_type=pl.DeviceIdType.MESH,
        )
        copy.start()
        sent.append(copy)

    def arrived(dst, send_sem, recv_sem, device):
        pltpu.make_async_remote_copy(
            src_ref=dst, dst_ref=dst, send_sem=send_sem, recv_sem=recv_sem,
            device_id=device, device_id_type=pl.DeviceIdType.MESH,
        ).wait_recv()

    loads = [
        pltpu.make_async_copy(src, dst, load_sem.at[i])
        for i, (src, dst) in enumerate(
            ((pool, pool_v), (gate_w, gate_v), (up_w, up_v), (down_w, down_v))
        )
    ]
    for copy in loads:
        copy.start()

    others = [lax.rem(dp + o, DP) for o in range(1, DP)]
    barrier = pltpu.get_barrier_semaphore()
    partners = [at_dp(rank) for rank in others]
    partners += [at_tp(z_at(o), l, c) for o in range(1, NZ)]
    partners += [at_tp(z, other_l, c), at_tp(z, l, other_c)]
    for device in partners:
        pl.semaphore_signal(barrier, inc=1, device_id=device, device_id_type=pl.DeviceIdType.MESH)
    pl.semaphore_wait(barrier, len(partners))

    def exchange(src_of, dst, s_sem, r_sem):
        for o, rank in enumerate(others):
            send(src_of(rank), dst.at[dp], s_sem.at[o], r_sem.at[o], at_dp(rank))

    def exchanged(dst, s_sem, r_sem):
        for o in range(DP - 1):
            rank = lax.rem(dp + (DP - 1 - o), DP)
            arrived(dst.at[rank], s_sem.at[o], r_sem.at[o], at_dp(rank))

    exchange(lambda rank: own.at[1, rank], route_a, a_s, a_r)
    route_a[dp] = own[1, dp]
    exchanged(route_a, a_s, a_r)
    picked = [route_a[plan[i]].astype(F32) for i in range(MIG)]
    fresh = picked[0][8:] + pltpu.roll(picked[1][8:], 1, 0) + pltpu.roll(picked[2][8:], 2, 0)
    b_send[...] = jnp.concatenate(
        [picked[0][:8], picked[1][:8], picked[2][:8], fresh], axis=0
    ).astype(BF)
    exchange(lambda rank: b_send, route_b, b_s, b_r)
    route_b[dp] = b_send[...]
    exchanged(route_b, b_s, b_r)

    serves = [plan[MIG + i] == dp for i in range(MIG)]
    local = own[0].astype(F32)
    listed = own[1].astype(F32)
    routed = route_b[...].astype(F32)
    row_q = listed[:, :8]
    row_new = listed[:, 8:9]
    for i in range(MIG):
        row_q = jnp.where(serves[i], routed[:, 8 * i : 8 * i + 8], row_q)
        row_new = jnp.where(serves[i], routed[:, 24 + i : 25 + i], row_new)
    upper = lax.broadcasted_iota(jnp.int32, (DP, 8, HD), 1) < 4
    q_tile = jnp.where(upper, local[:, :8], row_q)
    res_tile = jnp.where(upper, row_q, local[:, :8])
    res_tile = jnp.concatenate([res_tile[:, 4:], res_tile[:, :4]], axis=1)
    new_tile = jnp.where(
        upper,
        jnp.broadcast_to(local[:, 8:9], (DP, 8, HD)),
        jnp.broadcast_to(row_new, (DP, 8, HD)),
    )
    q_rows = q_tile.reshape(KVH, 16, HD)
    new_rows = jnp.concatenate([new_tile, new_tile], axis=1)
    new_keys, new_values = new_rows[:KVH], new_rows[KVH:]
    factor = 1.0 / math.sqrt(HD)
    new_score = jnp.sum(q_rows * new_keys, axis=-1, keepdims=True) * factor
    q_bf = q_rows.astype(BF)
    loads[0].wait()
    hidden_bias = bias[...]
    attended = []
    for head in range(KVH):
        keys = pool_v[:, head * HD : (head + 1) * HD]
        score = (
            lax.dot_general(
                q_bf[head], keys, (((1,), (1,)), ((), ())), preferred_element_type=F32
            )
            * factor
            + hidden_bias
        )
        own_score = new_score[head]
        top = jnp.maximum(jnp.max(score, axis=-1, keepdims=True), own_score)
        exponent = jnp.exp(score - top)
        own_exponent = jnp.exp(own_score - top)
        scale = 1.0 / (jnp.sum(exponent, axis=-1, keepdims=True) + own_exponent)
        weight = (exponent * scale).astype(BF)
        own_weight = (own_exponent * scale).astype(BF).astype(F32)
        values = pool_v[:, (KVH + head) * HD : (KVH + head + 1) * HD]
        attended.append(
            jnp.dot(weight, values, preferred_element_type=F32) + own_weight * new_values[head]
        )
    stream = res_tile + jnp.stack(attended).reshape(DP, 8, HD)
    square = jnp.sum(jnp.sum(stream * stream, axis=0), axis=-1, keepdims=True)
    first = lax.broadcasted_iota(jnp.int32, (8, 1), 0) < 4
    width = DP * 4 * HD
    total_0 = jnp.sum(jnp.where(first, square, 0.0), axis=0, keepdims=True)
    total_1 = jnp.sum(jnp.where(first, 0.0, square), axis=0, keepdims=True)
    mean = jnp.where(first, total_0, total_1) * (1.0 / width)
    normed = stream * lax.rsqrt(mean + EPSILON)[None] * gain[...]
    c_send[...] = jnp.concatenate([normed, stream], axis=1).astype(BF)
    exchange(lambda rank: c_send.at[rank], spread_c, c_s, c_r)
    spread_c[dp] = c_send[dp]
    exchanged(spread_c, c_s, c_r)

    tiles[...] = spread_c[:, :8].astype(F32).reshape(DP * 8, HD)
    x_all[z, c, l] = jnp.concatenate(
        [tiles[pl.ds(i, 32, stride=4), :] for i in range(4)], axis=1
    ).astype(BF)
    send(x_all.at[z, c, l], x_all.at[z, c, l], xl_s, xl_r, at_tp(z, other_l, c))
    arrived(x_all.at[z, c, other_l], xl_s, xl_r, at_tp(z, other_l, c))
    offsets = [o for chunk in CHUNKS for o in chunk]

    def slot(offset):
        return (offset + NZ) % NZ

    send(x_all.at[z, c], x_all.at[z, c], xc_s.at[0], xc_r.at[0], at_tp(z, l, other_c))
    for o in offsets[1:]:
        send(
            x_all.at[z, c], x_all.at[z, c], xz_s.at[slot(o)], xz_r.at[slot(o)],
            at_tp(z_at(-o), l, c),
        )

    def block_in(o):
        zz = z_at(o)
        arrived(x_all.at[zz, c], xz_s.at[slot(o)], xz_r.at[slot(o)], at_tp(zz, l, c))
        send(
            x_all.at[zz, c], x_all.at[zz, c], xc_s.at[slot(o)], xc_r.at[slot(o)],
            at_tp(z, l, other_c),
        )

    def block_whole(o):
        zz = z_at(o)
        arrived(x_all.at[zz, other_c], xc_s.at[slot(o)], xc_r.at[slot(o)], at_tp(z, l, other_c))

    right, left = at_x(xr), at_x(xl)

    def stage_in(q):
        for o in CHUNKS[q]:
            if o:
                block_in(o)

    def stage_a(q):
        for o in CHUNKS[q]:
            block_whole(o)
        rows = jnp.concatenate(
            [x_all[z_at(o)].reshape(128, 512) for o in CHUNKS[q]], axis=0
        )
        for weight, dst in ((gate_v, gate_p), (up_v, up_p)):
            value = jnp.dot(rows, weight[...], preferred_element_type=F32).astype(BF)
            value = value.reshape(2, NX, 2, 16, 512)
            for b in range(2):
                dst[q, :, 2 * b : 2 * b + 2] = value[b]
        send(gate_p.at[q, xo], m1g.at[q], xp_s.at[q, 0], xp_r.at[q, 0], right)
        send(up_p.at[q, xo], m1u.at[q], xp_s.at[q, 1], xp_r.at[q, 1], left)
        send(up_p.at[q, xr], m2u.at[q], xp_s.at[q, 2], xp_r.at[q, 2], right)
        send(gate_p.at[q, xl], m2g.at[q], xp_s.at[q, 3], xp_r.at[q, 3], left)

    def stage_b(q):
        arrived(m1g.at[q], xp_s.at[q, 0], xp_r.at[q, 0], left)
        s3g[q] = (gate_p[q, xr].astype(F32) + m1g[q].astype(F32)).astype(BF)
        send(s3g.at[q], m3g.at[q], xp_s.at[q, 4], xp_r.at[q, 4], right)
        arrived(m1u.at[q], xp_s.at[q, 1], xp_r.at[q, 1], right)
        s3u[q] = (up_p[q, xl].astype(F32) + m1u[q].astype(F32)).astype(BF)
        send(s3u.at[q], m3u.at[q], xp_s.at[q, 5], xp_r.at[q, 5], left)

    def stage_c(q):
        arrived(m2u.at[q], xp_s.at[q, 2], xp_r.at[q, 2], left)
        arrived(m2g.at[q], xp_s.at[q, 3], xp_r.at[q, 3], right)
        arrived(m3g.at[q], xp_s.at[q, 4], xp_r.at[q, 4], left)
        arrived(m3u.at[q], xp_s.at[q, 5], xp_r.at[q, 5], right)
        gate = gate_p[q, x].astype(F32) + m2g[q].astype(F32) + m3g[q].astype(F32)
        up = up_p[q, x].astype(F32) + m2u[q].astype(F32) + m3u[q].astype(F32)
        h_send[q, :, 0] = gate.astype(BF)
        h_send[q, :, 1] = up.astype(BF)
        for o in range(1, NH):
            place = lax.rem(h + o, NH)
            send(
                h_send.at[q, place], h_recv.at[q, o - 1],
                hp_s.at[q, o - 1], hp_r.at[q, o - 1], at_h(place),
            )

    def stage_d(q):
        for o in range(1, NH):
            arrived(
                h_recv.at[q, o - 1], hp_s.at[q, o - 1], hp_r.at[q, o - 1],
                at_h(lax.rem(h + NH - o, NH)),
            )
        total = h_send[q, h].astype(F32)
        for o in range(NH - 1):
            total = total + h_recv[q, o].astype(F32)
        gate, up = total[0], total[1]
        hid[q, x, h] = (gate / (1.0 + jnp.exp(-gate)) * up).astype(BF)
        for o in range(1, NH):
            send(
                hid.at[q, x, h], hid.at[q, x, h],
                hg_s.at[q, o - 1], hg_r.at[q, o - 1], at_h(lax.rem(h + o, NH)),
            )

    def stage_e(q):
        for o in range(1, NH):
            place = lax.rem(h + NH - o, NH)
            arrived(hid.at[q, x, place], hg_s.at[q, o - 1], hg_r.at[q, o - 1], at_h(place))
        send(hid.at[q, x], hid.at[q, x], xg_s.at[q, 0], xg_r.at[q, 0], right)
        send(hid.at[q, x], hid.at[q, x], xg_s.at[q, 1], xg_r.at[q, 1], left)

    def stage_f(q):
        arrived(hid.at[q, xl], xg_s.at[q, 0], xg_r.at[q, 0], left)
        half = hid.at[q, xl, pl.ds(0, 2)]
        send(half, half, xg_s.at[q, 2], xg_r.at[q, 2], right)
        arrived(hid.at[q, xr], xg_s.at[q, 1], xg_r.at[q, 1], right)
        half = hid.at[q, xr, pl.ds(2, 2)]
        send(half, half, xg_s.at[q, 3], xg_r.at[q, 3], left)

    def stage_g(q):
        arrived(hid.at[q, xo, pl.ds(0, 2)], xg_s.at[q, 2], xg_r.at[q, 2], left)
        arrived(hid.at[q, xo, pl.ds(2, 2)], xg_s.at[q, 3], xg_r.at[q, 3], right)
        rows = jnp.concatenate(
            [hid[q, :, 2 * b : 2 * b + 2].reshape(128, 512) for b in range(2)], axis=0
        )
        value = jnp.dot(rows, down_v[...], preferred_element_type=F32).astype(BF)
        value = value.reshape(2, 2, 2, 32, 512)
        for b in range(2):
            part[q, :, b] = value[b]
        send(part.at[q, other_c], part_in.at[q], oc_s.at[q], oc_r.at[q], at_tp(z, l, other_c))

    def stage_h(q):
        arrived(part_in.at[q], oc_s.at[q], oc_r.at[q], at_tp(z, l, other_c))
        z_send[q] = (part[q, c].astype(F32) + part_in[q].astype(F32)).astype(BF)
        for b, o in enumerate(CHUNKS[q]):
            if o:
                send(
                    z_send.at[q, b], z_recv.at[slot(o)], oz_s.at[slot(o)], oz_r.at[slot(o)],
                    at_tp(z_at(o), l, c),
                )

    stages = (stage_a, stage_b, stage_c, stage_d, stage_e, stage_f, stage_g, stage_h)
    stage_in(0)
    loads[1].wait()
    loads[2].wait()
    count, skew = len(CHUNKS), 2
    for step in range(skew * (count - 1) + len(stages)):
        for q in range(count):
            s = step - skew * q
            if 0 <= s < len(stages):
                if s == 0 and q:
                    pass
                if s == 6 and q == 0:
                    loads[3].wait()
                stages[s](q)
                if s == 0 and q + 1 < count:
                    stage_in(q + 1)

    total = z_send[0, 0].astype(F32)
    for o in offsets[1:]:
        arrived(z_recv.at[slot(o)], oz_s.at[slot(o)], oz_r.at[slot(o)], at_tp(z_at(-o), l, c))
        total = total + z_recv[slot(o)].astype(F32)
    l_send[...] = total.astype(BF)
    send(l_send.at[other_l], l_recv, ol_s, ol_r, at_tp(z, other_l, c))
    arrived(l_recv, ol_s, ol_r, at_tp(z, other_l, c))
    ffn = l_send[l].astype(F32) + l_recv[...].astype(F32)
    for i in range(4):
        tiles[pl.ds(i, 32, stride=4), :] = ffn[:, i * HD : (i + 1) * HD]
    finished = tiles[...].reshape(DP, 8, HD) + spread_c[:, 8:].astype(F32)
    e_recv[...] = finished
    upper_tile = lax.broadcasted_iota(jnp.int32, (8, HD), 0) < 4
    for rank in range(DP):
        e_send[rank] = jnp.where(upper_tile, e_recv[rank], e_recv[plan[2 * MIG + rank]])
    for o, rank in enumerate(others):
        send(e_send.at[rank], out.at[dp], e_s.at[o], e_r.at[o], at_dp(rank))
    out[dp] = e_send[dp]
    exchanged(out, e_s, e_r)
    for copy in sent:
        copy.wait_send()


def on_device(
    queries, residual, new_entries, page_pool, page_table, cache_lengths, migration,
    norm_gain, gate_weight, up_weight, down_weight,
):
    entries = migration[0]
    slot_id = entries[0, 0]
    second = slot_id == 1

    def ordered(value):
        return jnp.where(second, value, value[::-1])

    heads = ordered(queries[0, 0].reshape(2, DP, 4, HD))
    rest = ordered(residual[0, 0].reshape(2, DP, 4, HD))
    fresh = ordered(new_entries[0, 0].reshape(2, DP, 1, HD))
    blank = jnp.zeros((DP, 7, HD), BF)
    own = jnp.stack(
        [
            jnp.concatenate([heads[0], rest[0], fresh[0], blank], axis=1),
            jnp.concatenate([rest[1], heads[1], fresh[1], blank], axis=1),
        ]
    )
    table = ordered(page_table[0, 0])
    lengths = ordered(cache_lengths[0, 0])
    pages, page_rows = page_pool.shape[2], page_pool.shape[3]
    places = jnp.arange(table.shape[1], dtype=jnp.int32)
    held = jnp.clip(lengths[:, None] - page_rows * places[None, :], 0, page_rows)
    match = table[:, :, None] == jnp.arange(pages, dtype=jnp.int32)
    filled = jnp.sum(jnp.where(match, held[:, :, None], 0), axis=1)
    seen = jnp.arange(page_rows, dtype=jnp.int32)[None, None, :] < filled[:, :, None]
    bias = jnp.where(seen, 0.0, -1e30).astype(F32).reshape(1, 2, 1, pages * page_rows)
    bias = jnp.broadcast_to(bias, (2, 2, 4, pages * page_rows)).reshape(16, -1)
    gain = norm_gain.astype(F32).reshape(DP, 1, 4, HD)
    gain = jnp.broadcast_to(gain, (DP, 2, 4, HD)).reshape(DP, 8, HD)
    ranks = jnp.arange(DP, dtype=jnp.int32)
    anchors = ranks
    for i in range(MIG):
        anchors = jnp.where(ranks == entries[i, 2], entries[i, 1], anchors)
    plan = jnp.concatenate([entries[:, 2], entries[:, 1], anchors])

    vmem = pl.BlockSpec(memory_space=pltpu.VMEM)
    hbm = pl.BlockSpec(memory_space=pl.ANY)
    smem = pl.BlockSpec(memory_space=pltpu.SMEM)
    nq = len(CHUNKS)
    dma = pltpu.SemaphoreType.DMA
    share = (nq, NH, 16, 512)
    scratch = [
        pltpu.VMEM((512, 2048), BF),
        pltpu.VMEM((512, 512), BF), pltpu.VMEM((512, 512), BF), pltpu.VMEM((512, 512), BF),
        pltpu.VMEM((DP, 16, HD), BF), pltpu.VMEM((32, HD), BF), pltpu.VMEM((DP, 32, HD), BF),
        pltpu.VMEM((DP, 16, HD), BF), pltpu.VMEM((DP, 16, HD), BF),
        pltpu.VMEM((DP * 8, HD), F32),
        pltpu.VMEM((NZ, 2, 2, 32, 512), BF),
        pltpu.VMEM((nq, NX, NH, 16, 512), BF), pltpu.VMEM((nq, NX, NH, 16, 512), BF),
    ]
    scratch += [pltpu.VMEM(share, BF) for _ in range(8)]
    scratch += [
        pltpu.VMEM((nq, NH, 2, 16, 512), BF), pltpu.VMEM((nq, NH - 1, 2, 16, 512), BF),
        pltpu.VMEM((nq, NX, NH, 16, 512), BF),
        pltpu.VMEM((nq, 2, 2, 2, 32, 512), BF), pltpu.VMEM((nq, 2, 2, 32, 512), BF),
        pltpu.VMEM((nq, 2, 2, 32, 512), BF), pltpu.VMEM((NZ, 2, 32, 512), BF),
        pltpu.VMEM((2, 32, 512), BF), pltpu.VMEM((32, 512), BF),
        pltpu.VMEM((DP, 8, HD), F32), pltpu.VMEM((DP, 8, HD), F32),
    ]
    scratch += [dma((4,))]
    scratch += [dma((DP - 1,)) for _ in range(8)]
    scratch += [dma, dma, dma((NZ,)), dma((NZ,)), dma((NZ,)), dma((NZ,))]
    scratch += [dma((nq, 6)), dma((nq, 6)), dma((nq, 3)), dma((nq, 3)), dma((nq, 3)), dma((nq, 3))]
    scratch += [dma((nq, 4)), dma((nq, 4)), dma((nq,)), dma((nq,)), dma((NZ,)), dma((NZ,)), dma, dma]
    done = pl.pallas_call(
        kernel,
        out_shape=jax.ShapeDtypeStruct((DP, 8, HD), F32),
        in_specs=[smem, vmem, vmem, vmem, hbm, hbm, hbm, hbm],
        out_specs=vmem,
        scratch_shapes=scratch,
        compiler_params=pltpu.CompilerParams(
            collective_id=0, has_side_effects=True, vmem_limit_bytes=50 * 1024 * 1024
        ),
    )(
        plan, own, bias, gain, page_pool.reshape(pages * page_rows, page_pool.shape[4]),
        gate_weight, up_weight, down_weight,
    )
    done = jnp.where(second, done.reshape(DP, 2, 4, HD), done.reshape(DP, 2, 4, HD)[:, ::-1])
    return done.transpose(1, 0, 2, 3).astype(BF).reshape(1, 1, 2, DP * 4 * HD)


def solution(mesh):
    return jax.shard_map(
        on_device,
        mesh=mesh,
        in_specs=(
            P("dp", "tp", None, None),
            P("dp", "tp", None, None),
            P("dp", "tp", None, None),
            P("dp", "tp", None, None, None),
            P("dp", "tp", None, None),
            P("dp", "tp", None),
            P("tp", None, None),
            P(),
            P("dp", "tp"),
            P("dp", "tp"),
            P("tp", "dp"),
        ),
        out_specs=P("dp", "tp", None, None),
        check_vma=False,
    )
```

time: 629 us -> 141 us (0.22)
  waiting for transfers between devices: 493 us -> 0 us
  Pallas kernels: 0 us -> 121 us
  blocking collectives: 55.9 us -> 0 us
  between operations: 26.5 us -> 0.77 us
  other arithmetic: 14.2 us -> 5.47 us
  starting transfers between devices: 8.19 us -> 0 us
  matrix products: 8.08 us -> 0 us
  local copies, waits for them, and re-layouts: 18.7 us -> 11.8 us
    reduce_scatter x2 -> x0, waiting for transfers between devices: 205 us -> none  [the longest x1 115 us: on_device(): lax.psum_scatter(partial_value.astype(jnp.bfloat16), 'tp', scatter_dimens...]
    psum x1 -> x0, waiting for transfers between devices: 151 us -> none  [spread(): return lax.psum(kept, axis)]
    all_gather x2 -> x0, waiting for transfers between devices: 128 us -> none  [the longest x1 69 us: on_device(): gathered = lax.all_gather(pieces, 'tp', axis=0, tiled=True)]
    pallas_call x0 -> x1, Pallas kernels: none -> 121 us  [on_device(): pl.pallas_call(kernel, out_shape=jax.ShapeDtypeStruct((DP, 8, HD), F32),...]
    psum x1 -> x0, blocking collectives: 43.6 us -> none  [spread(): return lax.psum(kept, axis)]
    all_to_all x1 -> x0, blocking collectives: 12.3 us -> none  [on_device(): lax.all_to_all(normed, 'dp', split_axis=1, concat_axis=0, tiled=True)]
    all_to_all x1 -> x0, waiting for transfers between devices: 8.84 us -> none  [on_device(): lax.all_to_all(ffn, 'dp', split_axis=0, concat_axis=1, tiled=True)]
    dot_general x6 -> x0, matrix products: 8.08 us -> none  [the longest x1 2.91 us: on_device(): jnp.dot(lax.all_gather(hidden, 'dp', axis=0, tiled=True), down_weight, pr...]
  transfers between devices with their start and end apart: 6 -> 0, of which waited for: 6 -> 0; matrix products, arithmetic and copies ran while one was open for 1% -> 0% of each run, Pallas kernels for 0% -> 0%
where the time goes in v1:
time: 141 us; the launch traced here: 139 us
  Pallas kernels  121 us (86%)
  local copies, waits for them, and re-layouts  11.8 us (8%)
  other arithmetic  5.47 us (4%)
    pallas_call x1, Pallas kernels, on_device(): pl.pallas_call(kernel, out_shape=jax.ShapeDtypeStruct((DP, 8, HD), F32),...  121 us
    unnamed x10, local copies, waits for them, and re-layouts  6.1 us
    select_n x1, other arithmetic, on_device(): anchors = jnp.where(ranks == entries[i, 2], entries[i, 1], anchors)  3.71 us

profile of v1, /device:TPU:1, one launch (start us, length us, event | category | flops | bytes accessed | tf_op | source)
XLA Modules:
  0.0 138.6 jit_solution(13314310275435695025)
XLA Ops:
  0.0 0.7 rev.22
  0.8 0.1 pad.9.clone
  0.8 0.7 rev.21
  1.5 0.7 copy.27
  2.2 0.2 slice_reduce_fusion.1
  2.4 0.7 fusion.2
  3.8 0.7 broadcast_select_fusion
  4.4 0.8 subtract_clamp_fusion
  5.2 0.1 select_reduce_fusion
  5.3 3.7 %compare_select_fusion.3 = s32[16]{0:T(128)S(1)} fusion(s32[]{:T(128)} %bitcast.6, s32[]{:T(128)} %bitcast.5, s32[]{:T(128)} %bitcast.4, s32[]{:T(128)} %bitcast.3, s32[]{:T(128)} %bitcast.2, s32[]{:T(128)} %bitcast.1), kind=kLoop, calls=%fused_computation.24 | loop fusion | flops 96 | bytes 88 | tf_op jit(solution)/shard_map/jit(_where)/select_n | solution.py:378
  9.0 0.1 pad_add_fusion.plan
  9.1 0.7 copy.26
  9.8 0.1 lt.24
  9.9 0.1 lt.26
  10.0 0.1 lt.27
  10.1 0.8 reshape_squeeze.9
  10.9 0.8 reshape_squeeze.10
  11.8 0.1 maximum_bitcast_fusion
  11.9 0.7 broadcast_in_dim.66
  12.6 0.0 copy-start
  12.6 1.6 %copy-done = bf16[1,1,32,16,2048]{4,3,2,1,0:T(8,128)(2,1)S(1)} copy-done((bf16[1,1,32,16,2048]{4,3,2,1,0:T(8,128)(2,1)S(1)}, bf16[1,1,32,16,2048]{4,3,2,1,0:T(8,128)(2,1)}, u32[]{:S(2)}) %copy-start) | copy-done | bytes 2097176
  14.2 0.0 copy-start.1
  14.2 1.0 copy-done.1
  15.3 0.0 copy-start.2
  15.3 1.0 copy-done.2
  16.3 0.0 copy-start.3
  16.3 1.0 copy-done.3
  17.4 120.5 %shard_map.109 = f32[16,8,128]{2,1,0:T(8,128)S(1)} custom-call(s32[22]{0:T(128)S(1)} %pad_add_fusion.plan, bf16[2,16,16,128]{3,2,1,0:T(8,128)(2,1)S(1)} %pad_maximum_fusion.own, f32[16,512]{1,0:T(8,128)S(1)} %reshape.74.bias, f32[16,8,128]{2,1,0:T(8,128)S(1)} %bitcast.45, bf16[512,2048]{1,0:T(8,128)(2,1)S(1)} %bitcast.44, bf16[512,512]{1,0:T(8,128)(2,1)S(1)} %copy-done.1, ...), custom_call_target="tpu_custom_call" | custom-call | tf_op jit(solution)/shard_map/pallas_call | solution.py:410
  137.9 0.6 reshape.78
  (16 shorter events, 0.2 us)
Async XLA Ops:
  12.6 1.6 %copy-start = (bf16[1,1,32,16,2048]{4,3,2,1,0:T(8,128)(2,1)S(1)}, bf16[1,1,32,16,2048]{4,3,2,1,0:T(8,128)(2,1)}, u32[]{:S(2)}) copy-start(bf16[1,1,32,16,2048]{4,3,2,1,0:T(8,128)(2,1)} %param.14) | copy-start | bytes 6291460
  14.2 1.0 copy-start.1
  15.3 1.0 copy-start.2
  16.3 1.0 copy-start.3

commit v2 on v1

v2 whole, which is shorter than its diff:
```python
import math

import jax
import jax.numpy as jnp
from jax import lax
from jax.experimental import pallas as pl
from jax.experimental.pallas import tpu as pltpu
from jax.sharding import PartitionSpec as P

HD = 128
KVH = 8
NX, NH, NZ = 4, 4, 8
DP = NX * NH
MIG = 3
MAXP, PG = 16, 16
NEAR, FAR = (0, 1, -1, 2), (-2, -3, 3, 4)
CHUNKS = ((0, NEAR), (0, FAR), (1, FAR), (1, NEAR))
ORDER = (
    ("local", 0), ("x", 0), ("route", 0), ("y", 0), ("near", 0), ("a", 0), ("listed", 0),
    ("far", 0), ("b", 0), ("x", 1), ("a", 1), ("c", 0), ("y", 1), ("b", 1), ("far", 1), ("c", 1),
    ("a", 2), ("d", 0), ("near", 1), ("b", 2), ("a", 3), ("d", 1), ("c", 2), ("b", 3), ("e", 0),
    ("e", 1), ("c", 3), ("f", 0), ("d", 2), ("f", 1), ("g", 0), ("d", 3), ("g", 1), ("e", 2),
    ("h", 0), ("h", 1), ("f", 2), ("e", 3), ("g", 2), ("f", 3), ("h", 2), ("g", 3), ("h", 3),
)
EPSILON = 1e-05
BF = jnp.bfloat16
F32 = jnp.float32


def kernel(
    mig, table, lengths, q_in, res_in, new_in, gain, pool, gate_w, up_w, down_w, out,
    pool_v, gate_v, up_v, down_v,
    q_t, res_t, new_t, own, line, y_send, y_recv, c_send, spread_c, tiles, x_all,
    gate_p, up_p, m1g, m1u, m2g, m2u, s3g, s3u, m3g, m3u,
    h_send, h_recv, hid, part, part_in, z_send, z_recv, l_send, l_recv,
    fin, e_send, e_recv,
    load_sem, rx_s, rx_r, ry_s, ry_r, c_s, c_r, e_s, e_r,
    xl_s, xl_r, xz_s, xz_r, xc_s, xc_r,
    xp_s, xp_r, hp_s, hp_r, hg_s, hg_r, xg_s, xg_r,
    oc_s, oc_r, oz_s, oz_r, ol_s, ol_r,
):
    dp, tp = lax.axis_index("dp"), lax.axis_index("tp")
    h, x = lax.div(dp, NX), lax.rem(dp, NX)
    z, low = lax.div(tp, 4), lax.rem(tp, 4)
    l, c = lax.div(low, 2), lax.rem(low, 2)
    other_l, other_c = 1 - l, 1 - c
    xr, xo, xl = lax.rem(x + 1, NX), lax.rem(x + 2, NX), lax.rem(x + 3, NX)
    right, left = (h * NX + xr, tp), (h * NX + xl, tp)

    def at_dp(rank):
        return (rank, tp)

    def at_h(place):
        return (place * NX + x, tp)

    def at_tp(zz, ll, cc):
        return (dp, zz * 4 + ll * 2 + cc)

    def z_at(offset):
        return lax.rem(z + (offset + NZ), NZ)

    def slot(offset):
        return (offset + NZ) % NZ

    across_l, across_c = at_tp(z, other_l, c), at_tp(z, l, other_c)
    sent = []

    def send(src, dst, send_sem, recv_sem, device, listed_copy=True):
        copy = pltpu.make_async_remote_copy(
            src_ref=src, dst_ref=dst, send_sem=send_sem, recv_sem=recv_sem,
            device_id=device, device_id_type=pl.DeviceIdType.MESH,
        )
        copy.start()
        if listed_copy:
            sent.append(copy)

    def arrived(dst, send_sem, recv_sem, device):
        pltpu.make_async_remote_copy(
            src_ref=dst, dst_ref=dst, send_sem=send_sem, recv_sem=recv_sem,
            device_id=device, device_id_type=pl.DeviceIdType.MESH,
        ).wait_recv()

    loads = [
        pltpu.make_async_copy(src, dst, load_sem.at[i])
        for i, (src, dst) in enumerate(
            ((pool, pool_v), (gate_w, gate_v), (up_w, up_v), (down_w, down_v))
        )
    ]
    for copy in loads:
        copy.start()

    others = [lax.rem(dp + o, DP) for o in range(1, DP)]
    barrier = pltpu.get_barrier_semaphore()
    partners = [at_dp(rank) for rank in others]
    partners += [at_tp(z_at(o), l, c) for o in range(1, NZ)] + [across_l, across_c]
    for device in partners:
        pl.semaphore_signal(barrier, inc=1, device_id=device, device_id_type=pl.DeviceIdType.MESH)

    def exchange(src, dst, s_sem, r_sem):
        for rank in others:
            send(src.at[rank], dst.at[dp], s_sem, r_sem, at_dp(rank), False)
        dst[dp] = src[dp]

    def exchanged(dst, s_sem, r_sem):
        arrived(dst.at[pl.ds(0, DP - 1)], s_sem, r_sem, at_dp(others[0]))

    def all_left(src, s_sem, r_sem):
        part = src.at[pl.ds(0, DP - 1)]
        pltpu.make_async_remote_copy(
            src_ref=part, dst_ref=part, send_sem=s_sem, recv_sem=r_sem,
            device_id=at_dp(others[0]), device_id_type=pl.DeviceIdType.MESH,
        ).wait_send()

    slot_id = mig[0, 0]
    second = slot_id == 1

    def ordered(value):
        return jnp.where(second, value, jnp.concatenate([value[1:2], value[0:1]], axis=0))

    for source, dst, count in ((q_in, q_t, 64), (res_in, res_t, 64), (new_in, new_t, 16)):
        value = ordered(source[...].astype(F32))
        for j in range(count):
            dst[pl.ds(j, 2, stride=count), :] = value[:, j * HD : (j + 1) * HD]

    top_half = lax.broadcasted_iota(jnp.int32, (KVH, 8, HD), 1) < 4

    def turned(value):
        return jnp.concatenate([value[:, 4:], value[:, :4]], axis=1)

    def pieces(first, second_value):
        even = jnp.where(top_half, first, turned(second_value))
        odd = jnp.where(top_half, turned(first), second_value)
        return even, odd

    own[...] = jnp.concatenate([q_t[64:], res_t[64:], new_t[16:]], axis=0).astype(BF)

    def bias_of(place):
        lane = lax.broadcasted_iota(jnp.int32, (8, MAXP * 2 * PG), 1)
        page, inner = lane // PG, lane % PG
        length = lengths[place]
        filled = jnp.zeros_like(lane)
        for p in range(MAXP):
            held = jnp.minimum(jnp.maximum(length - p * PG, 0), PG)
            filled = jnp.where(page == table[place, p], held, filled)
        return jnp.where(inner < filled, 0.0, -1e30)

    def attend(w, q_rows, res_rows, new_rows, hidden_bias):
        factor = 1.0 / math.sqrt(HD)
        new_keys = jnp.stack([new_rows[j : j + 1] for j in range(KVH)])
        new_values = jnp.stack([new_rows[KVH + j : KVH + j + 1] for j in range(KVH)])
        q_bf = q_rows.astype(BF)
        score = jnp.stack(
            [
                lax.dot_general(
                    q_bf[head], pool_v[:, head * HD : (head + 1) * HD],
                    (((1,), (1,)), ((), ())), preferred_element_type=F32,
                )
                for head in range(KVH)
            ]
        )
        score = score * factor + hidden_bias[None]
        own_score = jnp.sum(q_rows * new_keys, axis=-1, keepdims=True) * factor
        top = jnp.maximum(jnp.max(score, axis=-1, keepdims=True), own_score)
        exponent = jnp.exp(score - top)
        own_exponent = jnp.exp(own_score - top)
        scale = 1.0 / (jnp.sum(exponent, axis=-1, keepdims=True) + own_exponent)
        weight = (exponent * scale).astype(BF)
        own_weight = (own_exponent * scale).astype(BF).astype(F32)
        attended = jnp.stack(
            [
                jnp.dot(
                    weight[head], pool_v[:, (KVH + head) * HD : (KVH + head + 1) * HD],
                    preferred_element_type=F32,
                )
                for head in range(KVH)
            ]
        )
        stream = res_rows + attended + own_weight * new_values
        square = jnp.sum(jnp.sum(stream * stream, axis=0), axis=-1, keepdims=True)
        mean = jnp.sum(square, axis=0, keepdims=True) * (1.0 / (DP * 4 * HD))
        scale = lax.rsqrt(mean + EPSILON)
        normed = stream * scale[None] * gain[...].astype(F32).reshape(KVH, 8, HD)
        even, odd = pieces(normed, stream)
        for k in range(DP):
            c_send[w, k] = (even, odd)[k % 2][k // 2]

    def spread(w):
        exchange(c_send.at[w], spread_c.at[w], c_s.at[w], c_r.at[w])

    def local(_):
        local_q = q_t[:64].reshape(KVH, 8, HD)
        local_res = res_t[:64].reshape(KVH, 8, HD)
        hidden_bias = bias_of(1 - slot_id)
        loads[0].wait()
        attend(0, local_q, local_res, new_t[:16], hidden_bias)
        pl.semaphore_wait(barrier, len(partners))
        spread(0)
        for o in range(1, NX):
            send(
                own, line.at[x], rx_s.at[o - 1], rx_r.at[o - 1],
                (h * NX + lax.rem(x + o, NX), tp),
            )
        line[x] = own[...]

    sources = [mig[i, 1] for i in range(MIG)]
    targets = [mig[i, 2] for i in range(MIG)]

    def route(_):
        for o in range(1, NX):
            place = lax.rem(x + NX - o, NX)
            arrived(line.at[place], rx_s.at[o - 1], rx_r.at[o - 1], (h * NX + place, tp))
        rows = [line[lax.rem(target, NX)].astype(F32) for target in targets]
        here = [lax.div(target, NX) == h for target in targets]

        def wanted(rank):
            value = jnp.zeros_like(rows[0])
            for i in range(MIG):
                value = jnp.where(here[i] & (sources[i] == rank), rows[i], value)
            return value.astype(BF)

        for o in range(1, NH):
            place = lax.rem(h + o, NH)
            y_send[o - 1] = wanted(place * NX + x)
            send(
                y_send.at[o - 1], y_recv.at[o - 1], ry_s.at[o - 1], ry_r.at[o - 1], at_h(place)
            )
        y_recv[NH - 1] = wanted(dp)

    def listed(_):
        for o in range(1, NH):
            arrived(
                y_recv.at[o - 1], ry_s.at[o - 1], ry_r.at[o - 1], at_h(lax.rem(h + NH - o, NH))
            )
        routed = y_recv[NH - 1].astype(F32)
        for o in range(NH - 1):
            routed = routed + y_recv[o].astype(F32)
        serves = (sources[0] == dp) | (sources[1] == dp) | (sources[2] == dp)
        row = jnp.where(serves, routed, own[...].astype(F32))
        attend(
            1, row[:64].reshape(KVH, 8, HD), row[64:128].reshape(KVH, 8, HD), row[128:],
            bias_of(slot_id),
        )
        spread(1)

    def start_x(w):
        exchanged(spread_c.at[w], c_s.at[w], c_r.at[w])
        tiles[...] = spread_c[w].reshape(DP * 8, HD)
        x_all[w, z, c, l] = jnp.concatenate(
            [tiles[pl.ds(i, DP, stride=8), :] for i in range(4)], axis=1
        ).astype(BF)
        block = x_all.at[w, z, c, l]
        send(block, block, xl_s.at[w], xl_r.at[w], across_l)

    def start_y(w):
        arrived(x_all.at[w, z, c, other_l], xl_s.at[w], xl_r.at[w], across_l)
        block = x_all.at[w, z, c]
        send(block, block, xc_s.at[w, 0], xc_r.at[w, 0], across_c)
        offsets = NEAR[1:] + FAR if w == 0 else FAR + NEAR[1:]
        for o in offsets:
            send(block, block, xz_s.at[w, slot(o)], xz_r.at[w, slot(o)], at_tp(z_at(-o), l, c))

    def forward(offsets):
        def run(w):
            for o in offsets:
                if o:
                    zz = z_at(o)
                    block = x_all.at[w, zz, c]
                    arrived(block, xz_s.at[w, slot(o)], xz_r.at[w, slot(o)], at_tp(zz, l, c))
                    send(block, block, xc_s.at[w, slot(o)], xc_r.at[w, slot(o)], across_c)

        return run

    def stage_a(q):
        w, offsets = CHUNKS[q]
        for o in offsets:
            arrived(x_all.at[w, z_at(o), other_c], xc_s.at[w, slot(o)], xc_r.at[w, slot(o)], across_c)
        if q == 0:
            loads[1].wait()
            loads[2].wait()
        rows = jnp.concatenate([x_all[w, z_at(o)].reshape(64, 512) for o in offsets], axis=0)
        for weight, dst in ((gate_v, gate_p), (up_v, up_p)):
            value = jnp.dot(rows, weight[...], preferred_element_type=F32).astype(BF)
            value = value.reshape(NH, NX, 16, 512)
            for b in range(NH):
                dst[q, :, b] = value[b]
        send(gate_p.at[q, xo], m1g.at[q], xp_s.at[q, 0], xp_r.at[q, 0], right)
        send(up_p.at[q, xo], m1u.at[q], xp_s.at[q, 1], xp_r.at[q, 1], left)
        send(up_p.at[q, xr], m2u.at[q], xp_s.at[q, 2], xp_r.at[q, 2], right)
        send(gate_p.at[q, xl], m2g.at[q], xp_s.at[q, 3], xp_r.at[q, 3], left)

    def stage_b(q):
        arrived(m1g.at[q], xp_s.at[q, 0], xp_r.at[q, 0], left)
        s3g[q] = (gate_p[q, xr].astype(F32) + m1g[q].astype(F32)).astype(BF)
        send(s3g.at[q], m3g.at[q], xp_s.at[q, 4], xp_r.at[q, 4], right)
        arrived(m1u.at[q], xp_s.at[q, 1], xp_r.at[q, 1], right)
        s3u[q] = (up_p[q, xl].astype(F32) + m1u[q].astype(F32)).astype(BF)
        send(s3u.at[q], m3u.at[q], xp_s.at[q, 5], xp_r.at[q, 5], left)

    def stage_c(q):
        arrived(m2u.at[q], xp_s.at[q, 2], xp_r.at[q, 2], left)
        arrived(m2g.at[q], xp_s.at[q, 3], xp_r.at[q, 3], right)
        arrived(m3g.at[q], xp_s.at[q, 4], xp_r.at[q, 4], left)
        arrived(m3u.at[q], xp_s.at[q, 5], xp_r.at[q, 5], right)
        gate = gate_p[q, x].astype(F32) + m2g[q].astype(F32) + m3g[q].astype(F32)
        up = up_p[q, x].astype(F32) + m2u[q].astype(F32) + m3u[q].astype(F32)
        h_send[q, :, 0] = gate.astype(BF)
        h_send[q, :, 1] = up.astype(BF)
        for o in range(1, NH):
            place = lax.rem(h + o, NH)
            send(
                h_send.at[q, place], h_recv.at[q, o - 1],
                hp_s.at[q, o - 1], hp_r.at[q, o - 1], at_h(place),
            )

    def stage_d(q):
        for o in range(1, NH):
            arrived(
                h_recv.at[q, o - 1], hp_s.at[q, o - 1], hp_r.at[q, o - 1],
                at_h(lax.rem(h + NH - o, NH)),
            )
        total = h_send[q, h].astype(F32)
        for o in range(NH - 1):
            total = total + h_recv[q, o].astype(F32)
        gate, up = total[0], total[1]
        hid[q, x, h] = (gate / (1.0 + jnp.exp(-gate)) * up).astype(BF)
        for o in range(1, NH):
            send(
                hid.at[q, x, h], hid.at[q, x, h],
                hg_s.at[q, o - 1], hg_r.at[q, o - 1], at_h(lax.rem(h + o, NH)),
            )

    def stage_e(q):
        for o in range(1, NH):
            place = lax.rem(h + NH - o, NH)
            arrived(hid.at[q, x, place], hg_s.at[q, o - 1], hg_r.at[q, o - 1], at_h(place))
        send(hid.at[q, x], hid.at[q, x], xg_s.at[q, 0], xg_r.at[q, 0], right)
        send(hid.at[q, x], hid.at[q, x], xg_s.at[q, 1], xg_r.at[q, 1], left)

    def stage_f(q):
        arrived(hid.at[q, xl], xg_s.at[q, 0], xg_r.at[q, 0], left)
        half = hid.at[q, xl, pl.ds(0, 2)]
        send(half, half, xg_s.at[q, 2], xg_r.at[q, 2], right)
        arrived(hid.at[q, xr], xg_s.at[q, 1], xg_r.at[q, 1], right)
        half = hid.at[q, xr, pl.ds(2, 2)]
        send(half, half, xg_s.at[q, 3], xg_r.at[q, 3], left)

    def stage_g(q):
        arrived(hid.at[q, xo, pl.ds(0, 2)], xg_s.at[q, 2], xg_r.at[q, 2], left)
        arrived(hid.at[q, xo, pl.ds(2, 2)], xg_s.at[q, 3], xg_r.at[q, 3], right)
        if q == 0:
            loads[3].wait()
        rows = jnp.concatenate([hid[q, :, b].reshape(64, 512) for b in range(NH)], axis=0)
        value = jnp.dot(rows, down_v[...], preferred_element_type=F32).astype(BF)
        value = value.reshape(NH, 2, 2, 16, 512)
        for b in range(NH):
            part[q, :, b] = value[b]
        send(part.at[q, other_c], part_in.at[q], oc_s.at[q], oc_r.at[q], across_c)

    def stage_h(q):
        w, offsets = CHUNKS[q]
        arrived(part_in.at[q], oc_s.at[q], oc_r.at[q], across_c)
        z_send[q] = (part[q, c].astype(F32) + part_in[q].astype(F32)).astype(BF)
        for b, o in enumerate(offsets):
            if o:
                send(
                    z_send.at[q, b], z_recv.at[w, slot(o)],
                    oz_s.at[w, slot(o)], oz_r.at[w, slot(o)], at_tp(z_at(o), l, c),
                )

    steps = {
        "local": local, "route": route, "listed": listed, "x": start_x, "y": start_y,
        "near": forward(NEAR), "far": forward(FAR), "a": stage_a, "b": stage_b, "c": stage_c,
        "d": stage_d, "e": stage_e, "f": stage_f, "g": stage_g, "h": stage_h,
    }
    for name, which in ORDER:
        steps[name](which)

    for w, q in ((0, 0), (1, 3)):
        total = z_send[q, 0].astype(F32)
        for o in FAR + NEAR[1:]:
            arrived(
                z_recv.at[w, slot(o)], oz_s.at[w, slot(o)], oz_r.at[w, slot(o)],
                at_tp(z_at(-o), l, c),
            )
            total = total + z_recv[w, slot(o)].astype(F32)
        l_send[:, w] = total.astype(BF)
    send(l_send.at[other_l], l_recv, ol_s, ol_r, across_l)
    arrived(l_recv, ol_s, ol_r, across_l)
    for w in range(2):
        ffn = l_send[l, w].astype(F32) + l_recv[w].astype(F32)
        for i in range(4):
            tiles[pl.ds(4 * w + i, DP, stride=8), :] = ffn[:, i * HD : (i + 1) * HD]
    first = lax.broadcasted_iota(jnp.int32, (DP, 8, HD), 1) < 4
    fin[...] = tiles[...].reshape(DP, 8, HD) + jnp.where(first, turned(spread_c[0]), spread_c[1])
    for rank in range(DP):
        anchor = jnp.int32(rank)
        for i in range(MIG):
            anchor = jnp.where(mig[i, 2] == rank, mig[i, 1], anchor)
        e_send[rank] = jnp.where(first[0], fin[rank], fin[anchor])
    exchange(e_send, e_recv, e_s, e_r)
    for w in range(2):
        all_left(c_send.at[w], c_s.at[w], c_r.at[w])
    for copy in sent:
        copy.wait_send()
    exchanged(e_recv, e_s, e_r)
    tiles[...] = e_recv[...].reshape(DP * 8, HD)
    value = jnp.concatenate(
        [tiles[pl.ds(k * 8 + i, 2, stride=4), :] for k in range(DP) for i in range(4)], axis=1
    )
    out[...] = ordered(value).astype(BF)
    all_left(e_send, e_s, e_r)


def on_device(
    queries, residual, new_entries, page_pool, page_table, cache_lengths, migration,
    norm_gain, gate_weight, up_weight, down_weight,
):
    pages, page_rows, entry = page_pool.shape[2:]
    vmem = pl.BlockSpec(memory_space=pltpu.VMEM)
    hbm = pl.BlockSpec(memory_space=pl.ANY)
    smem = pl.BlockSpec(memory_space=pltpu.SMEM)
    nq = len(CHUNKS)
    dma = pltpu.SemaphoreType.DMA
    share = (nq, NH, 16, 512)
    scratch = [
        pltpu.VMEM((512, 2048), BF),
        pltpu.VMEM((512, 512), BF), pltpu.VMEM((512, 512), BF), pltpu.VMEM((512, 512), BF),
        pltpu.VMEM((128, HD), F32), pltpu.VMEM((128, HD), F32), pltpu.VMEM((32, HD), F32),
        pltpu.VMEM((144, HD), BF), pltpu.VMEM((NX, 144, HD), BF),
        pltpu.VMEM((NH - 1, 144, HD), BF), pltpu.VMEM((NH, 144, HD), BF),
        pltpu.VMEM((2, DP, 8, HD), F32), pltpu.VMEM((2, DP, 8, HD), F32),
        pltpu.VMEM((DP * 8, HD), F32),
        pltpu.VMEM((2, NZ, 2, 2, 16, 512), BF),
        pltpu.VMEM((nq, NX, NH, 16, 512), BF), pltpu.VMEM((nq, NX, NH, 16, 512), BF),
    ]
    scratch += [pltpu.VMEM(share, BF) for _ in range(8)]
    scratch += [
        pltpu.VMEM((nq, NH, 2, 16, 512), BF), pltpu.VMEM((nq, NH - 1, 2, 16, 512), BF),
        pltpu.VMEM((nq, NX, NH, 16, 512), BF),
        pltpu.VMEM((nq, 2, NH, 2, 16, 512), BF), pltpu.VMEM((nq, NH, 2, 16, 512), BF),
        pltpu.VMEM((nq, NH, 2, 16, 512), BF), pltpu.VMEM((2, NZ, 2, 16, 512), BF),
        pltpu.VMEM((2, 2, 16, 512), BF), pltpu.VMEM((2, 16, 512), BF),
        pltpu.VMEM((DP, 8, HD), F32), pltpu.VMEM((DP, 8, HD), F32), pltpu.VMEM((DP, 8, HD), F32),
    ]
    scratch += [dma((4,))]
    scratch += [dma((3,)) for _ in range(4)]
    scratch += [dma((2,)), dma((2,)), dma, dma]
    scratch += [dma((2,)), dma((2,)), dma((2, NZ)), dma((2, NZ)), dma((2, NZ)), dma((2, NZ))]
    scratch += [dma((nq, 6)), dma((nq, 6)), dma((nq, 3)), dma((nq, 3)), dma((nq, 3)), dma((nq, 3))]
    scratch += [dma((nq, 4)), dma((nq, 4)), dma((nq,)), dma((nq,)), dma((2, NZ)), dma((2, NZ)), dma, dma]
    done = pl.pallas_call(
        kernel,
        out_shape=jax.ShapeDtypeStruct((2, DP * 4 * HD), BF),
        in_specs=[smem, smem, smem, vmem, vmem, vmem, vmem, hbm, hbm, hbm, hbm],
        out_specs=vmem,
        scratch_shapes=scratch,
        compiler_params=pltpu.CompilerParams(
            collective_id=0, has_side_effects=True, vmem_limit_bytes=62 * 1024 * 1024
        ),
    )(
        migration[0], page_table[0, 0], cache_lengths[0, 0],
        queries[0, 0], residual[0, 0], new_entries[0, 0], norm_gain.reshape(DP * 4, HD),
        page_pool.reshape(pages * page_rows, entry), gate_weight, up_weight, down_weight,
    )
    return done.reshape(1, 1, 2, DP * 4 * HD)


def solution(mesh):
    return jax.shard_map(
        on_device,
        mesh=mesh,
        in_specs=(
            P("dp", "tp", None, None),
            P("dp", "tp", None, None),
            P("dp", "tp", None, None),
            P("dp", "tp", None, None, None),
            P("dp", "tp", None, None),
            P("dp", "tp", None),
            P("tp", None, None),
            P(),
            P("dp", "tp"),
            P("dp", "tp"),
            P("tp", "dp"),
        ),
        out_specs=P("dp", "tp", None, None),
        check_vma=False,
    )
```

time: 141 us -> 102 us (0.72)
  Pallas kernels: 121 us -> 97.6 us
  local copies, waits for them, and re-layouts: 11.8 us -> 2.65 us
  other arithmetic: 5.47 us -> 0 us
    pallas_call x1, Pallas kernels: 121 us -> 97.6 us  [on_device(): pl.pallas_call(kernel, out_shape=jax.ShapeDtypeStruct((2, DP * 4 * HD), B...]
    select_n x5 -> x0, other arithmetic: 4.42 us -> none  [the longest x1 3.71 us: on_device(): anchors = jnp.where(ranks == entries[i, 2], entries[i, 1], anchors)]
    unnamed x10 -> x2, local copies, waits for them, and re-layouts: 6.1 us -> 2.65 us
    another operation x2 -> x0, local copies, waits for them, and re-layouts: 1.59 us -> none  [the longest x1 0.79 us: on_device(): heads = ordered(queries[0, 0].reshape(2, DP, 4, HD))]
    rev x2 -> x0, local copies, waits for them, and re-layouts: 1.45 us -> none  [ordered(): return jnp.where(second, value, value[::-1])]
where the time goes in v2:
time: 102 us; the launch traced here: 100 us
  Pallas kernels  97.6 us (96%)
  local copies, waits for them, and re-layouts  2.65 us (3%)
    pallas_call x1, Pallas kernels, on_device(): pl.pallas_call(kernel, out_shape=jax.ShapeDtypeStruct((2, DP * 4 * HD), B...  97.6 us
    unnamed x2, local copies, waits for them, and re-layouts  2.65 us

profile of v2, /device:TPU:1, one launch (start us, length us, event | category | flops | bytes accessed | tf_op | source)
XLA Modules:
  0.0 100.3 jit_solution(4810296852532087843)
XLA Ops:
  0.0 1.3 %copy.14 = s32[1,3,3]{2,1,0:T(4,128)} copy(s32[1,3,3]{2,0,1:T(1,128)} %param.17) | data formatting | bytes 72
  1.3 97.6 %shard_map.109 = bf16[2,8192]{1,0:T(2,128)(2,1)} custom-call(s32[3,3]{1,0:T(4,128)} %bitcast.17, s32[2,16]{1,0:T(2,128)} %bitcast.18, s32[2]{0:T(128)} %bitcast.19, bf16[2,8192]{1,0:T(2,128)(2,1)} %bitcast.13, bf16[2,8192]{1,0:T(2,128)(2,1)} %bitcast.14, bf16[2,2048]{1,0:T(2,128)(2,1)} %bitcast.16, bf16[64,128]{1,0:T(8,128)(2,1)} %bitcast.15, ...), custom_call_target="tpu_custom_call" | custom-call | tf_op jit(solution)/shard_map/pallas_call | solution.py:451
  98.9 1.4 %copy.16 = bf16[1,1,2,8192]{3,2,1,0:T(2,128)(2,1)} copy(bf16[1,1,2,8192]{3,2,1,0:T(2,128)(2,1)} %bitcast.12) | data formatting | bytes 65536

commit v3 on v2

v3 whole, which is shorter than its diff:
```python
import math

import jax
import jax.numpy as jnp
from jax import lax
from jax.experimental import pallas as pl
from jax.experimental.pallas import tpu as pltpu
from jax.sharding import PartitionSpec as P

HD = 128
KVH = 8
NX, NH, NZ = 4, 4, 8
DP = NX * NH
MIG = 3
MAXP, PG = 16, 16
CHUNKS = (
    (0, (0, 1)), (0, (-1, 2)), (0, (-2, 3)), (0, (-3, 4)),
    (1, (-3, 4)), (1, (-2, 3)), (1, (-1, 2)), (1, (0, 1)),
)
SIZES = [16 * len(offsets) for _, offsets in CHUNKS]
STARTS = [sum(SIZES[:q]) for q in range(len(CHUNKS))]
ORDER = (
    "local", "x0", "route", "y0", "w0", "w1", "a0", "listed", "b0", "w2", "a1", "x1", "a2", "w3",
    "b1", "y1", "c0", "a3", "c1", "b2", "b3", "d0", "w4", "w5", "c2", "a4", "w6", "w7", "d1",
    "a5", "c3", "b4", "a7", "d2", "b5", "e0", "c4", "a6", "d3", "e1", "c5", "e2", "b6", "f0",
    "b7", "d4", "f1", "f2", "e3", "c6", "d5", "c7", "g2", "e4", "g0", "g1", "f3", "d6", "h2",
    "e5", "f4", "h0", "g3", "h1", "d7", "e6", "h3", "g4", "f5", "e7", "f6", "h4", "g5", "f7",
    "g6", "h5", "l0", "g7", "h6", "h7", "m0", "l1", "m1",
)
DISTANCES = (10, 9, 11, 8, 6, 14, 2, 5, 7, 13, 15, 4, 12, 1, 3)
EPSILON = 1e-05
BF = jnp.bfloat16
F32 = jnp.float32


def kernel(
    mig, table, lengths, q_in, res_in, new_in, gain, pool, gate_w, up_w, down_w, out,
    pool_v, gate_v, up_v, down_v,
    q_t, res_t, new_t, own, line, y_send, y_recv, c_local, c_listed, in_local, in_listed,
    stream_local, tiles, x_all,
    gate_p, up_p, m1g, m1u, m2g, m2u, s3g, s3u, m3g, m3u,
    h_send, h_recv, hid, part, part_in, z_send, z_recv, l_send, l_recv,
    rows_out, fin, e_send, e_recv,
    load_sem, rx_s, rx_r, ry_s, ry_r, c_s, c_r, e_s, e_r,
    xl_s, xl_r, xz_s, xz_r, xc_s, xc_r,
    xp_s, xp_r, hp_s, hp_r, hg_s, hg_r, xg_s, xg_r,
    oc_s, oc_r, oz_s, oz_r, ol_s, ol_r,
):
    dp, tp = lax.axis_index("dp"), lax.axis_index("tp")
    h, x = lax.div(dp, NX), lax.rem(dp, NX)
    z, low = lax.div(tp, 4), lax.rem(tp, 4)
    l, c = lax.div(low, 2), lax.rem(low, 2)
    other_l, other_c = 1 - l, 1 - c
    xr, xo, xl = lax.rem(x + 1, NX), lax.rem(x + 2, NX), lax.rem(x + 3, NX)
    right, left = (h * NX + xr, tp), (h * NX + xl, tp)

    def at_dp(rank):
        return (rank, tp)

    def at_h(place):
        return (place * NX + x, tp)

    def at_tp(zz, ll, cc):
        return (dp, zz * 4 + ll * 2 + cc)

    def z_at(offset):
        return lax.rem(z + (offset + NZ), NZ)

    def slot(offset):
        return (offset + NZ) % NZ

    across_l, across_c = at_tp(z, other_l, c), at_tp(z, l, other_c)
    sent = []

    def send(src, dst, send_sem, recv_sem, device, listed_copy=True):
        copy = pltpu.make_async_remote_copy(
            src_ref=src, dst_ref=dst, send_sem=send_sem, recv_sem=recv_sem,
            device_id=device, device_id_type=pl.DeviceIdType.MESH,
        )
        copy.start()
        if listed_copy:
            sent.append(copy)

    def arrived(dst, send_sem, recv_sem, device):
        pltpu.make_async_remote_copy(
            src_ref=dst, dst_ref=dst, send_sem=send_sem, recv_sem=recv_sem,
            device_id=device, device_id_type=pl.DeviceIdType.MESH,
        ).wait_recv()

    loads = [
        pltpu.make_async_copy(src, dst, load_sem.at[i])
        for i, (src, dst) in enumerate(
            ((pool, pool_v), (gate_w, gate_v), (up_w, up_v), (down_w, down_v))
        )
    ]
    for copy in loads:
        copy.start()
    waiting = set(range(len(loads)))

    def use(i):
        if i in waiting:
            waiting.discard(i)
            loads[i].wait()


    others = [lax.rem(h + o // NX, NH) * NX + lax.rem(x + o % NX, NX) for o in DISTANCES]
    barrier = pltpu.get_barrier_semaphore()
    partners = [at_dp(rank) for rank in others]
    partners += [at_tp(z_at(o), l, c) for o in range(1, NZ)] + [across_l, across_c]
    for device in partners:
        pl.semaphore_signal(barrier, inc=1, device_id=device, device_id_type=pl.DeviceIdType.MESH)

    def exchange(src, dst, s_sem, r_sem):
        for rank in others:
            send(src.at[rank], dst.at[dp], s_sem, r_sem, at_dp(rank), False)
        dst[dp] = src[dp]

    def exchanged(dst, s_sem, r_sem):
        arrived(dst.at[pl.ds(0, DP - 1)], s_sem, r_sem, at_dp(others[0]))

    def all_left(src, s_sem, r_sem):
        part = src.at[pl.ds(0, DP - 1)]
        pltpu.make_async_remote_copy(
            src_ref=part, dst_ref=part, send_sem=s_sem, recv_sem=r_sem,
            device_id=at_dp(others[0]), device_id_type=pl.DeviceIdType.MESH,
        ).wait_send()

    slot_id = mig[0, 0, 0]
    second = slot_id == 1

    def ordered(value):
        return jnp.where(second, value, jnp.concatenate([value[1:2], value[0:1]], axis=0))

    for source, dst, count in ((q_in, q_t, 64), (res_in, res_t, 64), (new_in, new_t, 16)):
        value = ordered(source[...].astype(F32))
        for j in range(count):
            dst[pl.ds(j, 2, stride=count), :] = value[:, j * HD : (j + 1) * HD]

    top_half = lax.broadcasted_iota(jnp.int32, (KVH, 8, HD), 1) < 4

    def turned(value):
        return jnp.concatenate([value[:, 4:], value[:, :4]], axis=1)

    def pieces(first, second_value):
        even = jnp.where(top_half, first, turned(second_value))
        odd = jnp.where(top_half, turned(first), second_value)
        return even, odd

    own[...] = jnp.concatenate([q_t[64:], res_t[64:], new_t[16:]], axis=0).astype(BF)

    def bias_of(place):
        lane = lax.broadcasted_iota(jnp.int32, (8, MAXP * 2 * PG), 1)
        page, inner = lane // PG, lane % PG
        length = lengths[place]
        filled = jnp.zeros_like(lane)
        for p in range(MAXP):
            held = jnp.minimum(jnp.maximum(length - p * PG, 0), PG)
            filled = jnp.where(page == table[place, p], held, filled)
        return jnp.where(inner < filled, 0.0, -1e30)

    def attend(q_rows, res_rows, new_rows, hidden_bias):
        factor = 1.0 / math.sqrt(HD)
        new_keys = jnp.stack([new_rows[j : j + 1] for j in range(KVH)])
        new_values = jnp.stack([new_rows[KVH + j : KVH + j + 1] for j in range(KVH)])
        q_bf = q_rows.astype(BF)
        score = jnp.stack(
            [
                lax.dot_general(
                    q_bf[head], pool_v[:, head * HD : (head + 1) * HD],
                    (((1,), (1,)), ((), ())), preferred_element_type=F32,
                )
                for head in range(KVH)
            ]
        )
        score = score * factor + hidden_bias[None]
        own_score = jnp.sum(q_rows * new_keys, axis=-1, keepdims=True) * factor
        top = jnp.maximum(jnp.max(score, axis=-1, keepdims=True), own_score)
        exponent = jnp.exp(score - top)
        own_exponent = jnp.exp(own_score - top)
        scale = 1.0 / (jnp.sum(exponent, axis=-1, keepdims=True) + own_exponent)
        weight = (exponent * scale).astype(BF)
        own_weight = (own_exponent * scale).astype(BF).astype(F32)
        attended = jnp.stack(
            [
                jnp.dot(
                    weight[head], pool_v[:, (KVH + head) * HD : (KVH + head + 1) * HD],
                    preferred_element_type=F32,
                )
                for head in range(KVH)
            ]
        )
        stream = res_rows + attended + own_weight * new_values
        square = jnp.sum(jnp.sum(stream * stream, axis=0), axis=-1, keepdims=True)
        mean = jnp.sum(square, axis=0, keepdims=True) * (1.0 / (DP * 4 * HD))
        scale = lax.rsqrt(mean + EPSILON)
        normed = stream * scale[None] * gain[...].astype(F32).reshape(KVH, 8, HD)
        return normed, stream

    def local(_):
        local_q = q_t[:64].reshape(KVH, 8, HD)
        local_res = res_t[:64].reshape(KVH, 8, HD)
        hidden_bias = bias_of(1 - slot_id)
        use(0)
        normed, stream = attend(local_q, local_res, new_t[:16], hidden_bias)
        stream_local[...] = stream.reshape(DP * 4, HD)
        for k in range(DP):
            c_local[k] = normed[k // 2, 4 * (k % 2) : 4 * (k % 2) + 4]
        pl.semaphore_wait(barrier, len(partners))
        exchange(c_local, in_local, c_s.at[0], c_r.at[0])
        for o in range(1, NX):
            send(
                own, line.at[x], rx_s.at[o - 1], rx_r.at[o - 1],
                (h * NX + lax.rem(x + o, NX), tp),
            )
        line[x] = own[...]

    sources = [mig[i, 0, 1] for i in range(MIG)]
    targets = [mig[i, 0, 2] for i in range(MIG)]

    def route(_):
        for o in range(1, NX):
            place = lax.rem(x + NX - o, NX)
            arrived(line.at[place], rx_s.at[o - 1], rx_r.at[o - 1], (h * NX + place, tp))
        rows = [line[lax.rem(target, NX)].astype(F32) for target in targets]
        here = [lax.div(target, NX) == h for target in targets]

        def wanted(rank):
            value = jnp.zeros_like(rows[0])
            for i in range(MIG):
                value = jnp.where(here[i] & (sources[i] == rank), rows[i], value)
            return value.astype(BF)

        for o in range(1, NH):
            place = lax.rem(h + o, NH)
            y_send[o - 1] = wanted(place * NX + x)
            send(
                y_send.at[o - 1], y_recv.at[o - 1], ry_s.at[o - 1], ry_r.at[o - 1], at_h(place)
            )
        y_recv[NH - 1] = wanted(dp)

    def listed(_):
        for o in range(1, NH):
            arrived(
                y_recv.at[o - 1], ry_s.at[o - 1], ry_r.at[o - 1], at_h(lax.rem(h + NH - o, NH))
            )
        routed = y_recv[NH - 1].astype(F32)
        for o in range(NH - 1):
            routed = routed + y_recv[o].astype(F32)
        serves = (sources[0] == dp) | (sources[1] == dp) | (sources[2] == dp)
        row = jnp.where(serves, routed, own[...].astype(F32))
        normed, stream = attend(
            row[:64].reshape(KVH, 8, HD), row[64:128].reshape(KVH, 8, HD), row[128:],
            bias_of(slot_id),
        )
        even, odd = pieces(normed, stream)
        for k in range(DP):
            c_listed[k] = (even, odd)[k % 2][k // 2]
        exchange(c_listed, in_listed, c_s.at[1], c_r.at[1])

    def start_x(w):
        source, count = (in_local, 4) if w == 0 else (in_listed, 8)
        exchanged(source, c_s.at[w], c_r.at[w])
        for a in range(DP):
            tiles[count * a : count * a + count] = source[a]
        x_all[w, z, c, l] = jnp.concatenate(
            [tiles[pl.ds(i, DP, stride=count), :] for i in range(4)], axis=1
        ).astype(BF)
        block = x_all.at[w, z, c, l]
        send(block, block, xl_s.at[w], xl_r.at[w], across_l)

    def start_y(w):
        arrived(x_all.at[w, z, c, other_l], xl_s.at[w], xl_r.at[w], across_l)
        block = x_all.at[w, z, c]
        send(block, block, xc_s.at[w, 0], xc_r.at[w, 0], across_c)
        offsets = [o for kind, places in CHUNKS if kind == w for o in places if o]
        for o in offsets:
            send(block, block, xz_s.at[w, slot(o)], xz_r.at[w, slot(o)], at_tp(z_at(-o), l, c))

    def forward(q):
        w, offsets = CHUNKS[q]
        for o in offsets:
            if o:
                zz = z_at(o)
                block = x_all.at[w, zz, c]
                arrived(block, xz_s.at[w, slot(o)], xz_r.at[w, slot(o)], at_tp(zz, l, c))
                send(block, block, xc_s.at[w, slot(o)], xc_r.at[w, slot(o)], across_c)

    def span(q):
        return pl.ds(STARTS[q], SIZES[q])

    def stage_a(q):
        w, offsets = CHUNKS[q]
        for o in offsets:
            arrived(x_all.at[w, z_at(o), other_c], xc_s.at[w, slot(o)], xc_r.at[w, slot(o)], across_c)
        use(1)
        use(2)
        rows = jnp.concatenate([x_all[w, z_at(o)].reshape(64, 512) for o in offsets], axis=0)
        part_rows = span(q)
        for weight, dst in ((gate_v, gate_p), (up_v, up_p)):
            value = jnp.dot(rows, weight[...], preferred_element_type=F32).astype(BF)
            dst[:, part_rows] = value.reshape(NX, SIZES[q], 512)
        send(gate_p.at[xo, part_rows], m1g.at[part_rows], xp_s.at[q, 0], xp_r.at[q, 0], right)
        send(up_p.at[xo, part_rows], m1u.at[part_rows], xp_s.at[q, 1], xp_r.at[q, 1], left)
        send(up_p.at[xr, part_rows], m2u.at[part_rows], xp_s.at[q, 2], xp_r.at[q, 2], right)
        send(gate_p.at[xl, part_rows], m2g.at[part_rows], xp_s.at[q, 3], xp_r.at[q, 3], left)

    def stage_b(q):
        t = span(q)
        arrived(m1g.at[t], xp_s.at[q, 0], xp_r.at[q, 0], left)
        s3g[t] = (gate_p[xr, t].astype(F32) + m1g[t].astype(F32)).astype(BF)
        send(s3g.at[t], m3g.at[t], xp_s.at[q, 4], xp_r.at[q, 4], right)
        arrived(m1u.at[t], xp_s.at[q, 1], xp_r.at[q, 1], right)
        s3u[t] = (up_p[xl, t].astype(F32) + m1u[t].astype(F32)).astype(BF)
        send(s3u.at[t], m3u.at[t], xp_s.at[q, 5], xp_r.at[q, 5], left)

    def stage_c(q):
        t = span(q)
        arrived(m2u.at[t], xp_s.at[q, 2], xp_r.at[q, 2], left)
        arrived(m2g.at[t], xp_s.at[q, 3], xp_r.at[q, 3], right)
        arrived(m3g.at[t], xp_s.at[q, 4], xp_r.at[q, 4], left)
        arrived(m3u.at[t], xp_s.at[q, 5], xp_r.at[q, 5], right)
        gate = gate_p[x, t].astype(F32) + m2g[t].astype(F32) + m3g[t].astype(F32)
        up = up_p[x, t].astype(F32) + m2u[t].astype(F32) + m3u[t].astype(F32)
        gate, up = gate.astype(BF), up.astype(BF)
        for b in range(NH):
            columns = slice(b * HD, (b + 1) * HD)
            h_send[b, t] = jnp.concatenate([gate[:, columns], up[:, columns]], axis=1)
        for o in (2, 1, 3):
            place = lax.rem(h + o, NH)
            send(
                h_send.at[place, t], h_recv.at[o - 1, t],
                hp_s.at[q, o - 1], hp_r.at[q, o - 1], at_h(place),
            )

    def stage_d(q):
        t = span(q)
        for o in range(1, NH):
            arrived(
                h_recv.at[o - 1, t], hp_s.at[q, o - 1], hp_r.at[q, o - 1],
                at_h(lax.rem(h + NH - o, NH)),
            )
        total = h_send[h, t].astype(F32)
        for o in range(NH - 1):
            total = total + h_recv[o, t].astype(F32)
        gate, up = total[:, :HD], total[:, HD:]
        hid[x, h, t] = (gate / (1.0 + jnp.exp(-gate)) * up).astype(BF)
        block = hid.at[x, h, t]
        for o in (2, 1, 3):
            send(
                block, block, hg_s.at[q, o - 1], hg_r.at[q, o - 1], at_h(lax.rem(h + o, NH))
            )

    def stage_e(q):
        t = span(q)
        for o in range(1, NH):
            place = lax.rem(h + NH - o, NH)
            arrived(hid.at[x, place, t], hg_s.at[q, o - 1], hg_r.at[q, o - 1], at_h(place))
        block = hid.at[x, pl.ds(0, NH), t]
        send(block, block, xg_s.at[q, 0], xg_r.at[q, 0], right)
        send(block, block, xg_s.at[q, 1], xg_r.at[q, 1], left)

    def stage_f(q):
        t = span(q)
        arrived(hid.at[xl, pl.ds(0, NH), t], xg_s.at[q, 0], xg_r.at[q, 0], left)
        half = hid.at[xl, pl.ds(0, 2), t]
        send(half, half, xg_s.at[q, 2], xg_r.at[q, 2], right)
        arrived(hid.at[xr, pl.ds(0, NH), t], xg_s.at[q, 1], xg_r.at[q, 1], right)
        half = hid.at[xr, pl.ds(2, 2), t]
        send(half, half, xg_s.at[q, 3], xg_r.at[q, 3], left)

    def stage_g(q):
        t = span(q)
        arrived(hid.at[xo, pl.ds(0, 2), t], xg_s.at[q, 2], xg_r.at[q, 2], left)
        arrived(hid.at[xo, pl.ds(2, 2), t], xg_s.at[q, 3], xg_r.at[q, 3], right)
        use(3)
        rows = jnp.concatenate(
            [jnp.concatenate([hid[a, b, t] for b in range(NH)], axis=1) for a in range(NX)], axis=0
        )
        value = jnp.dot(rows, down_v[...], preferred_element_type=F32).astype(BF)
        count, first_block = SIZES[q] // 16, STARTS[q] // 16
        value = value.reshape(count, 2, 2, 16, 512)
        for b in range(count):
            part[:, first_block + b] = value[b]
        blocks = pl.ds(first_block, count)
        send(part.at[other_c, blocks], part_in.at[blocks], oc_s.at[q], oc_r.at[q], across_c)

    def stage_h(q):
        w, offsets = CHUNKS[q]
        first_block = STARTS[q] // 16
        blocks = pl.ds(first_block, SIZES[q] // 16)
        arrived(part_in.at[blocks], oc_s.at[q], oc_r.at[q], across_c)
        z_send[blocks] = (part[c, blocks].astype(F32) + part_in[blocks].astype(F32)).astype(BF)
        for b, o in enumerate(offsets):
            if o:
                send(
                    z_send.at[first_block + b], z_recv.at[w, slot(o)],
                    oz_s.at[w, slot(o)], oz_r.at[w, slot(o)], at_tp(z_at(o), l, c),
                )

    def start_l(w):
        offsets = []
        for q, (kind, places) in enumerate(CHUNKS):
            for b, o in enumerate(places):
                if kind == w and o:
                    offsets.append(o)
                elif kind == w:
                    total = z_send[STARTS[q] // 16 + b].astype(F32)
        for o in offsets:
            arrived(
                z_recv.at[w, slot(o)], oz_s.at[w, slot(o)], oz_r.at[w, slot(o)],
                at_tp(z_at(-o), l, c),
            )
            total = total + z_recv[w, slot(o)].astype(F32)
        l_send[w] = total.astype(BF)
        send(l_send.at[w, other_l], l_recv.at[w], ol_s.at[w], ol_r.at[w], across_l)

    def start_m(w):
        arrived(l_recv.at[w], ol_s.at[w], ol_r.at[w], across_l)
        ffn = l_send[w, l].astype(F32) + l_recv[w].astype(F32)
        for i in range(4):
            rows_out[w, pl.ds(i, DP, stride=4), :] = ffn[:, i * HD : (i + 1) * HD]
        if w == 0:
            for rank in range(DP):
                e_send[0, rank] = rows_out[0, 4 * rank : 4 * rank + 4]
        else:
            for rank in range(DP):
                fin[rank] = rows_out[1, 4 * rank : 4 * rank + 4] + in_listed[rank, 4:]
            for rank in range(DP):
                anchor = jnp.int32(rank)
                for i in range(MIG):
                    anchor = jnp.where(targets[i] == rank, sources[i], anchor)
                e_send[1, rank] = fin[anchor]
        exchange(e_send.at[w], e_recv.at[w], e_s.at[w], e_r.at[w])

    steps = {
        "local": local, "route": route, "listed": listed, "x": start_x, "y": start_y,
        "w": forward, "a": stage_a, "b": stage_b, "c": stage_c, "d": stage_d, "e": stage_e,
        "f": stage_f, "g": stage_g, "h": stage_h, "l": start_l, "m": start_m,
    }
    for step in ORDER:
        name = step.rstrip("0123456789")
        steps[name](int(step[len(name) :] or 0))

    all_left(c_local, c_s.at[0], c_r.at[0])
    all_left(c_listed, c_s.at[1], c_r.at[1])
    for copy in sent:
        copy.wait_send()
    for w in range(2):
        exchanged(e_recv.at[w], e_s.at[w], e_r.at[w])
        for k in range(DP):
            tiles[64 * w + 4 * k : 64 * w + 4 * k + 4] = e_recv[w, k]
    tiles[:64] = tiles[:64] + stream_local[...]
    value = jnp.concatenate([tiles[pl.ds(j, 2, stride=64), :] for j in range(64)], axis=1)
    out[...] = ordered(value).astype(BF)
    for w in range(2):
        all_left(e_send.at[w], e_s.at[w], e_r.at[w])


def on_device(
    queries, residual, new_entries, page_pool, page_table, cache_lengths, migration,
    norm_gain, gate_weight, up_weight, down_weight,
):
    pages, page_rows, entry = page_pool.shape[2:]
    vmem = pl.BlockSpec(memory_space=pltpu.VMEM)
    hbm = pl.BlockSpec(memory_space=pl.ANY)
    smem = pl.BlockSpec(memory_space=pltpu.SMEM)
    nq = len(CHUNKS)
    dma = pltpu.SemaphoreType.DMA
    share = (256, 512)
    scratch = [
        pltpu.VMEM((512, 2048), BF),
        pltpu.VMEM((512, 512), BF), pltpu.VMEM((512, 512), BF), pltpu.VMEM((512, 512), BF),
        pltpu.VMEM((128, HD), F32), pltpu.VMEM((128, HD), F32), pltpu.VMEM((32, HD), F32),
        pltpu.VMEM((144, HD), BF), pltpu.VMEM((NX, 144, HD), BF),
        pltpu.VMEM((NH - 1, 144, HD), BF), pltpu.VMEM((NH, 144, HD), BF),
        pltpu.VMEM((DP, 4, HD), F32), pltpu.VMEM((DP, 8, HD), F32),
        pltpu.VMEM((DP, 4, HD), F32), pltpu.VMEM((DP, 8, HD), F32),
        pltpu.VMEM((64, HD), F32), pltpu.VMEM((DP * 8, HD), F32),
        pltpu.VMEM((2, NZ, 2, 2, 16, 512), BF),
        pltpu.VMEM((NX,) + share, BF), pltpu.VMEM((NX,) + share, BF),
    ]
    scratch += [pltpu.VMEM(share, BF) for _ in range(8)]
    scratch += [
        pltpu.VMEM((NH, 256, 256), BF), pltpu.VMEM((NH - 1, 256, 256), BF),
        pltpu.VMEM((NX, NH, 256, HD), BF),
        pltpu.VMEM((2, 16, 2, 16, 512), BF), pltpu.VMEM((16, 2, 16, 512), BF),
        pltpu.VMEM((16, 2, 16, 512), BF), pltpu.VMEM((2, NZ, 2, 16, 512), BF),
        pltpu.VMEM((2, 2, 16, 512), BF), pltpu.VMEM((2, 16, 512), BF),
        pltpu.VMEM((2, 64, HD), F32), pltpu.VMEM((DP, 4, HD), F32),
        pltpu.VMEM((2, DP, 4, HD), F32), pltpu.VMEM((2, DP, 4, HD), F32),
    ]
    scratch += [dma((4,))]
    scratch += [dma((3,)) for _ in range(4)]
    scratch += [dma((2,)), dma((2,)), dma((2,)), dma((2,))]
    scratch += [dma((2,)), dma((2,)), dma((2, NZ)), dma((2, NZ)), dma((2, NZ)), dma((2, NZ))]
    scratch += [dma((nq, 6)), dma((nq, 6)), dma((nq, 3)), dma((nq, 3)), dma((nq, 3)), dma((nq, 3))]
    scratch += [dma((nq, 4)), dma((nq, 4)), dma((nq,)), dma((nq,)), dma((2, NZ)), dma((2, NZ))]
    scratch += [dma((2,)), dma((2,))]
    done = pl.pallas_call(
        kernel,
        out_shape=jax.ShapeDtypeStruct((2, DP * 4 * HD), BF),
        in_specs=[smem, smem, smem, vmem, vmem, vmem, vmem, hbm, hbm, hbm, hbm],
        out_specs=vmem,
        scratch_shapes=scratch,
        compiler_params=pltpu.CompilerParams(
            collective_id=0, has_side_effects=True, vmem_limit_bytes=62 * 1024 * 1024
        ),
    )(
        migration.transpose(1, 0, 2), page_table[0, 0], cache_lengths[0, 0],
        queries[0, 0], residual[0, 0], new_entries[0, 0], norm_gain.reshape(DP * 4, HD),
        page_pool.reshape(pages * page_rows, entry), gate_weight, up_weight, down_weight,
    )
    return done.reshape(1, 1, 2, DP * 4 * HD)


def solution(mesh):
    return jax.shard_map(
        on_device,
        mesh=mesh,
        in_specs=(
            P("dp", "tp", None, None),
            P("dp", "tp", None, None),
            P("dp", "tp", None, None),
            P("dp", "tp", None, None, None),
            P("dp", "tp", None, None),
            P("dp", "tp", None),
            P("tp", None, None),
            P(),
            P("dp", "tp"),
            P("dp", "tp"),
            P("tp", "dp"),
        ),
        out_specs=P("dp", "tp", None, None),
        check_vma=False,
    )
```

time: 102 us -> 97.8 us (0.959)
  Pallas kernels: 97.6 us -> 95.1 us
  local copies, waits for them, and re-layouts: 2.65 us -> 1.4 us
    pallas_call x1, Pallas kernels: 97.6 us -> 95.1 us  [on_device(): pl.pallas_call(kernel, out_shape=jax.ShapeDtypeStruct((2, DP * 4 * HD), B...]
    unnamed x2 -> x1, local copies, waits for them, and re-layouts: 2.65 us -> 1.4 us
where the time goes in v3:
time: 97.8 us; the launch traced here: 96.5 us
  Pallas kernels  95.1 us (97%)
  local copies, waits for them, and re-layouts  1.4 us (1%)
    pallas_call x1, Pallas kernels, on_device(): pl.pallas_call(kernel, out_shape=jax.ShapeDtypeStruct((2, DP * 4 * HD), B...  95.1 us

profile of v3, /device:TPU:1, one launch (start us, length us, event | category | flops | bytes accessed | tf_op | source)
XLA Modules:
  0.0 96.5 jit_solution(6211639064676200036)
XLA Ops:
  0.0 95.1 %shard_map.109 = bf16[2,8192]{1,0:T(2,128)(2,1)} custom-call(s32[3,1,3]{2,1,0:T(1,128)} %bitcast.15, s32[2,16]{1,0:T(2,128)} %bitcast.16, s32[2]{0:T(128)} %bitcast.17, bf16[2,8192]{1,0:T(2,128)(2,1)} %bitcast.11, bf16[2,8192]{1,0:T(2,128)(2,1)} %bitcast.12, bf16[2,2048]{1,0:T(2,128)(2,1)} %bitcast.14, bf16[64,128]{1,0:T(8,128)(2,1)} %bitcast.13, ...), custom_call_target="tpu_custom_call" | custom-call | tf_op jit(solution)/shard_map/pallas_call | solution.py:499
  95.1 1.4 %copy.13 = bf16[1,1,2,8192]{3,2,1,0:T(2,128)(2,1)} copy(bf16[1,1,2,8192]{3,2,1,0:T(2,128)(2,1)} %bitcast.10) | data formatting | bytes 65536

commit v4 on v3

--- a/solution.py
+++ b/solution.py
@@ -13,19 +13,19 @@
 DP = NX * NH
 MIG = 3
 MAXP, PG = 16, 16
+PLACES = (0, 1, -1, 2, -2, 3, -3, 4)
 CHUNKS = (
-    (0, (0, 1)), (0, (-1, 2)), (0, (-2, 3)), (0, (-3, 4)),
-    (1, (-3, 4)), (1, (-2, 3)), (1, (-1, 2)), (1, (0, 1)),
+    (0, (0, 1)), (0, (-1, 2, -2, 3)), (0, (-3, 4)), (1, (-3, 4)), (1, (-1, 2, -2, 3)),
+    (1, (0, 1)),
 )
-SIZES = [16 * len(offsets) for _, offsets in CHUNKS]
+SIZES = [8 * len(offsets) for _, offsets in CHUNKS]
 STARTS = [sum(SIZES[:q]) for q in range(len(CHUNKS))]
 ORDER = (
-    "local", "x0", "route", "y0", "w0", "w1", "a0", "listed", "b0", "w2", "a1", "x1", "a2", "w3",
-    "b1", "y1", "c0", "a3", "c1", "b2", "b3", "d0", "w4", "w5", "c2", "a4", "w6", "w7", "d1",
-    "a5", "c3", "b4", "a7", "d2", "b5", "e0", "c4", "a6", "d3", "e1", "c5", "e2", "b6", "f0",
-    "b7", "d4", "f1", "f2", "e3", "c6", "d5", "c7", "g2", "e4", "g0", "g1", "f3", "d6", "h2",
-    "e5", "f4", "h0", "g3", "h1", "d7", "e6", "h3", "g4", "f5", "e7", "f6", "h4", "g5", "f7",
-    "g6", "h5", "l0", "g7", "h6", "h7", "m0", "l1", "m1",
+    "local", "x0", "route", "y0", "r01", "listed", "r02", "a0", "x1", "r03", "c0", "y1", "a1",
+    "r04", "r11", "d0", "a2", "r12", "c1", "a5", "r13", "c2", "e0", "a4", "r14", "c5", "d2", "d1",
+    "a3", "c4", "e2", "f0", "e1", "d5", "c3", "f2", "g0", "f1", "d4", "g2", "d3", "e5", "h0",
+    "e4", "h2", "e3", "g1", "f3", "f4", "f5", "h1", "g3", "g4", "h3", "g5", "h4", "l0", "h5",
+    "m0", "l1", "m1",
 )
 DISTANCES = (10, 9, 11, 8, 6, 14, 2, 5, 7, 13, 15, 4, 12, 1, 3)
 EPSILON = 1e-05
@@ -35,14 +35,13 @@
 
 def kernel(
     mig, table, lengths, q_in, res_in, new_in, gain, pool, gate_w, up_w, down_w, out,
-    pool_v, gate_v, up_v, down_v,
+    pool_v, weight, down_v,
     q_t, res_t, new_t, own, line, y_send, y_recv, c_local, c_listed, in_local, in_listed,
     stream_local, tiles, x_all,
-    gate_p, up_p, m1g, m1u, m2g, m2u, s3g, s3u, m3g, m3u,
-    h_send, h_recv, hid, part, part_in, z_send, z_recv, l_send, l_recv,
+    sums, sums_in, h_send, h_recv, hid, part, part_in, z_send, z_recv, l_send, l_recv,
     rows_out, fin, e_send, e_recv,
     load_sem, rx_s, rx_r, ry_s, ry_r, c_s, c_r, e_s, e_r,
-    xl_s, xl_r, xz_s, xz_r, xc_s, xc_r,
+    w_s, w_r, xl_s, xl_r, xz_s, xz_r, xc_s, xc_r,
     xp_s, xp_r, hp_s, hp_r, hg_s, hg_r, xg_s, xg_r,
     oc_s, oc_r, oz_s, oz_r, ol_s, ol_r,
 ):
@@ -51,8 +50,11 @@
     z, low = lax.div(tp, 4), lax.rem(tp, 4)
     l, c = lax.div(low, 2), lax.rem(low, 2)
     other_l, other_c = 1 - l, 1 - c
-    xr, xo, xl = lax.rem(x + 1, NX), lax.rem(x + 2, NX), lax.rem(x + 3, NX)
-    right, left = (h * NX + xr, tp), (h * NX + xl, tp)
+    parity, side = lax.rem(x, 2), lax.div(x, 2)
+    half = lax.rem(lax.div(x + 1, 2), 2)
+    mate, like = x + 1 - 2 * parity, NX - 1 - x
+    other_side, opposite = 1 - side, NX - 1 - mate
+    at_mate, at_like = (h * NX + mate, tp), (h * NX + like, tp)
 
     def at_dp(rank):
         return (rank, tp)
@@ -87,15 +89,23 @@
             device_id=device, device_id_type=pl.DeviceIdType.MESH,
         ).wait_recv()
 
+    def columns_of(array, which):
+        return array.at[:, pl.ds(pl.multiple_of(which * 256, 256), 256)]
+
     loads = [
         pltpu.make_async_copy(src, dst, load_sem.at[i])
         for i, (src, dst) in enumerate(
-            ((pool, pool_v), (gate_w, gate_v), (up_w, up_v), (down_w, down_v))
+            (
+                (pool, pool_v),
+                (columns_of(gate_w, half), weight.at[parity, :, pl.ds(0, 256)]),
+                (columns_of(up_w, half), weight.at[parity, :, pl.ds(256, 256)]),
+                (down_w, down_v),
+            )
         )
     ]
     for copy in loads:
         copy.start()
-    waiting = set(range(len(loads)))
+    waiting = set(range(len(loads) + 1))
 
     def use(i):
         if i in waiting:
@@ -110,10 +120,11 @@
     for device in partners:
         pl.semaphore_signal(barrier, inc=1, device_id=device, device_id_type=pl.DeviceIdType.MESH)
 
-    def exchange(src, dst, s_sem, r_sem):
+    def exchange(src, dst, s_sem, r_sem, share=1):
         for rank in others:
-            send(src.at[rank], dst.at[dp], s_sem, r_sem, at_dp(rank), False)
-        dst[dp] = src[dp]
+            part = src.at[lax.div(rank, share)] if share > 1 else src.at[rank]
+            send(part, dst.at[dp], s_sem, r_sem, at_dp(rank), False)
+        dst[dp] = src[lax.div(dp, share)] if share > 1 else src[dp]
 
     def exchanged(dst, s_sem, r_sem):
         arrived(dst.at[pl.ds(0, DP - 1)], s_sem, r_sem, at_dp(others[0]))
@@ -135,16 +146,6 @@
         value = ordered(source[...].astype(F32))
         for j in range(count):
             dst[pl.ds(j, 2, stride=count), :] = value[:, j * HD : (j + 1) * HD]
-
-    top_half = lax.broadcasted_iota(jnp.int32, (KVH, 8, HD), 1) < 4
-
-    def turned(value):
-        return jnp.concatenate([value[:, 4:], value[:, :4]], axis=1)
-
-    def pieces(first, second_value):
-        even = jnp.where(top_half, first, turned(second_value))
-        odd = jnp.where(top_half, turned(first), second_value)
-        return even, odd
 
     own[...] = jnp.concatenate([q_t[64:], res_t[64:], new_t[16:]], axis=0).astype(BF)
 
@@ -203,16 +204,18 @@
         use(0)
         normed, stream = attend(local_q, local_res, new_t[:16], hidden_bias)
         stream_local[...] = stream.reshape(DP * 4, HD)
-        for k in range(DP):
-            c_local[k] = normed[k // 2, 4 * (k % 2) : 4 * (k % 2) + 4]
+        c_local[...] = normed
         pl.semaphore_wait(barrier, len(partners))
-        exchange(c_local, in_local, c_s.at[0], c_r.at[0])
+        exchange(c_local, in_local, c_s.at[0], c_r.at[0], 2)
         for o in range(1, NX):
             send(
                 own, line.at[x], rx_s.at[o - 1], rx_r.at[o - 1],
                 (h * NX + lax.rem(x + o, NX), tp),
             )
         line[x] = own[...]
+        for i, array in enumerate((gate_w, up_w)):
+            dst = weight.at[parity, :, pl.ds(256 * i, 256)]
+            send(columns_of(array, 1 - half), dst, w_s.at[i], w_r.at[i], at_mate)
 
     sources = [mig[i, 0, 1] for i in range(MIG)]
     targets = [mig[i, 0, 2] for i in range(MIG)]
@@ -252,79 +255,76 @@
             row[:64].reshape(KVH, 8, HD), row[64:128].reshape(KVH, 8, HD), row[128:],
             bias_of(slot_id),
         )
-        even, odd = pieces(normed, stream)
-        for k in range(DP):
-            c_listed[k] = (even, odd)[k % 2][k // 2]
-        exchange(c_listed, in_listed, c_s.at[1], c_r.at[1])
+        c_listed[...] = jnp.concatenate([normed, stream], axis=1).astype(BF)
+        exchange(c_listed, in_listed, c_s.at[1], c_r.at[1], 2)
 
     def start_x(w):
-        source, count = (in_local, 4) if w == 0 else (in_listed, 8)
+        source = in_local if w == 0 else in_listed
         exchanged(source, c_s.at[w], c_r.at[w])
-        for a in range(DP):
-            tiles[count * a : count * a + count] = source[a]
-        x_all[w, z, c, l] = jnp.concatenate(
-            [tiles[pl.ds(i, DP, stride=count), :] for i in range(4)], axis=1
+        rows = source[...] if w == 0 else source[:, :8].astype(F32)
+        tiles[...] = rows.reshape(DP * 8, HD)
+        x_all[w, 0, c, l] = jnp.concatenate(
+            [tiles[pl.ds(i, DP, stride=8), :] for i in range(8)], axis=1
         ).astype(BF)
-        block = x_all.at[w, z, c, l]
+        block = x_all.at[w, 0, c, l]
         send(block, block, xl_s.at[w], xl_r.at[w], across_l)
 
+    def place_of(w, o):
+        return x_all.at[w, PLACES.index(o), c]
+
+    def pass_on(w, o):
+        for step, device in ((1, at_tp(z_at(-1), l, c)), (-1, at_tp(z_at(1), l, c))):
+            to = o + step
+            if (o == 0 or o * step > 0) and to in PLACES:
+                send(
+                    place_of(w, o), place_of(w, to),
+                    xz_s.at[w, slot(to)], xz_r.at[w, slot(to)], device,
+                )
+
     def start_y(w):
-        arrived(x_all.at[w, z, c, other_l], xl_s.at[w], xl_r.at[w], across_l)
-        block = x_all.at[w, z, c]
-        send(block, block, xc_s.at[w, 0], xc_r.at[w, 0], across_c)
-        offsets = [o for kind, places in CHUNKS if kind == w for o in places if o]
-        for o in offsets:
-            send(block, block, xz_s.at[w, slot(o)], xz_r.at[w, slot(o)], at_tp(z_at(-o), l, c))
-
-    def forward(q):
-        w, offsets = CHUNKS[q]
-        for o in offsets:
-            if o:
-                zz = z_at(o)
-                block = x_all.at[w, zz, c]
-                arrived(block, xz_s.at[w, slot(o)], xz_r.at[w, slot(o)], at_tp(zz, l, c))
-                send(block, block, xc_s.at[w, slot(o)], xc_r.at[w, slot(o)], across_c)
-
-    def span(q):
-        return pl.ds(STARTS[q], SIZES[q])
+        arrived(x_all.at[w, 0, c, other_l], xl_s.at[w], xl_r.at[w], across_l)
+        pass_on(w, 0)
+
+    def ring(code):
+        w, i = code // 10, code % 10
+        for o in (i, -i):
+            if o in PLACES:
+                source = at_tp(z_at(1 if o > 0 else -1), l, c)
+                arrived(place_of(w, o), xz_s.at[w, slot(o)], xz_r.at[w, slot(o)], source)
+                pass_on(w, o)
+        blocks = x_all.at[w, pl.ds(2 * i - 2, 2), c]
+        send(blocks, blocks, xc_s.at[w, i - 1], xc_r.at[w, i - 1], across_c)
+
+    def span(q, count=1):
+        return pl.ds(STARTS[q] * count, SIZES[q] * count)
 
     def stage_a(q):
         w, offsets = CHUNKS[q]
-        for o in offsets:
-            arrived(x_all.at[w, z_at(o), other_c], xc_s.at[w, slot(o)], xc_r.at[w, slot(o)], across_c)
+        first, count = PLACES.index(offsets[0]), len(offsets)
+        for i in range(first // 2, (first + count) // 2):
+            blocks = x_all.at[w, pl.ds(2 * i, 2), other_c]
+            arrived(blocks, xc_s.at[w, i], xc_r.at[w, i], across_c)
         use(1)
         use(2)
-        rows = jnp.concatenate([x_all[w, z_at(o)].reshape(64, 512) for o in offsets], axis=0)
-        part_rows = span(q)
-        for weight, dst in ((gate_v, gate_p), (up_v, up_p)):
-            value = jnp.dot(rows, weight[...], preferred_element_type=F32).astype(BF)
-            dst[:, part_rows] = value.reshape(NX, SIZES[q], 512)
-        send(gate_p.at[xo, part_rows], m1g.at[part_rows], xp_s.at[q, 0], xp_r.at[q, 0], right)
-        send(up_p.at[xo, part_rows], m1u.at[part_rows], xp_s.at[q, 1], xp_r.at[q, 1], left)
-        send(up_p.at[xr, part_rows], m2u.at[part_rows], xp_s.at[q, 2], xp_r.at[q, 2], right)
-        send(gate_p.at[xl, part_rows], m2g.at[part_rows], xp_s.at[q, 3], xp_r.at[q, 3], left)
-
-    def stage_b(q):
+        if 4 in waiting:
+            waiting.discard(4)
+            for i in range(2):
+                dst = weight.at[1 - parity, :, pl.ds(256 * i, 256)]
+                arrived(dst, w_s.at[i], w_r.at[i], at_mate)
+        rows = x_all[w, first : first + count].reshape(64 * count, 1024)
+        value = jnp.dot(
+            rows, weight[...].reshape(1024, 512), preferred_element_type=F32
+        ).astype(BF)
+        t = span(q, 4)
+        sums[:, t] = value.reshape(2, 4 * SIZES[q], 512)
+        send(sums.at[other_side, t], sums_in.at[t], xp_s.at[q], xp_r.at[q], at_like)
+
+    def stage_c(q):
+        t = span(q, 4)
+        arrived(sums_in.at[t], xp_s.at[q], xp_r.at[q], at_like)
+        value = (sums[side, t].astype(F32) + sums_in[t].astype(F32)).astype(BF)
         t = span(q)
-        arrived(m1g.at[t], xp_s.at[q, 0], xp_r.at[q, 0], left)
-        s3g[t] = (gate_p[xr, t].astype(F32) + m1g[t].astype(F32)).astype(BF)
-        send(s3g.at[t], m3g.at[t], xp_s.at[q, 4], xp_r.at[q, 4], right)
-        arrived(m1u.at[t], xp_s.at[q, 1], xp_r.at[q, 1], right)
-        s3u[t] = (up_p[xl, t].astype(F32) + m1u[t].astype(F32)).astype(BF)
-        send(s3u.at[t], m3u.at[t], xp_s.at[q, 5], xp_r.at[q, 5], left)
-
-    def stage_c(q):
-        t = span(q)
-        arrived(m2u.at[t], xp_s.at[q, 2], xp_r.at[q, 2], left)
-        arrived(m2g.at[t], xp_s.at[q, 3], xp_r.at[q, 3], right)
-        arrived(m3g.at[t], xp_s.at[q, 4], xp_r.at[q, 4], left)
-        arrived(m3u.at[t], xp_s.at[q, 5], xp_r.at[q, 5], right)
-        gate = gate_p[x, t].astype(F32) + m2g[t].astype(F32) + m3g[t].astype(F32)
-        up = up_p[x, t].astype(F32) + m2u[t].astype(F32) + m3u[t].astype(F32)
-        gate, up = gate.astype(BF), up.astype(BF)
-        for b in range(NH):
-            columns = slice(b * HD, (b + 1) * HD)
-            h_send[b, t] = jnp.concatenate([gate[:, columns], up[:, columns]], axis=1)
+        h_send[:, t] = value.reshape(NH, SIZES[q], 512)
         for o in (2, 1, 3):
             place = lax.rem(h + o, NH)
             send(
@@ -342,7 +342,7 @@
         total = h_send[h, t].astype(F32)
         for o in range(NH - 1):
             total = total + h_recv[o, t].astype(F32)
-        gate, up = total[:, :HD], total[:, HD:]
+        gate, up = total[:, :256], total[:, 256:]
         hid[x, h, t] = (gate / (1.0 + jnp.exp(-gate)) * up).astype(BF)
         block = hid.at[x, h, t]
         for o in (2, 1, 3):
@@ -356,28 +356,29 @@
             place = lax.rem(h + NH - o, NH)
             arrived(hid.at[x, place, t], hg_s.at[q, o - 1], hg_r.at[q, o - 1], at_h(place))
         block = hid.at[x, pl.ds(0, NH), t]
-        send(block, block, xg_s.at[q, 0], xg_r.at[q, 0], right)
-        send(block, block, xg_s.at[q, 1], xg_r.at[q, 1], left)
+        send(block, block, xg_s.at[q, 0], xg_r.at[q, 0], at_like)
+        send(block, block, xg_s.at[q, 1], xg_r.at[q, 1], at_mate)
 
     def stage_f(q):
-        t = span(q)
-        arrived(hid.at[xl, pl.ds(0, NH), t], xg_s.at[q, 0], xg_r.at[q, 0], left)
-        half = hid.at[xl, pl.ds(0, 2), t]
-        send(half, half, xg_s.at[q, 2], xg_r.at[q, 2], right)
-        arrived(hid.at[xr, pl.ds(0, NH), t], xg_s.at[q, 1], xg_r.at[q, 1], right)
-        half = hid.at[xr, pl.ds(2, 2), t]
-        send(half, half, xg_s.at[q, 3], xg_r.at[q, 3], left)
+        block = hid.at[like, pl.ds(0, NH), span(q)]
+        arrived(block, xg_s.at[q, 0], xg_r.at[q, 0], at_like)
+        send(block, block, xg_s.at[q, 2], xg_r.at[q, 2], at_mate)
 
     def stage_g(q):
         t = span(q)
-        arrived(hid.at[xo, pl.ds(0, 2), t], xg_s.at[q, 2], xg_r.at[q, 2], left)
-        arrived(hid.at[xo, pl.ds(2, 2), t], xg_s.at[q, 3], xg_r.at[q, 3], right)
+        for i, place in ((1, mate), (2, opposite)):
+            arrived(hid.at[place, pl.ds(0, NH), t], xg_s.at[q, i], xg_r.at[q, i], at_mate)
         use(3)
         rows = jnp.concatenate(
-            [jnp.concatenate([hid[a, b, t] for b in range(NH)], axis=1) for a in range(NX)], axis=0
+            [
+                jnp.concatenate([hid[first, b, t], hid[second_half, b, t]], axis=1)
+                for first, second_half in ((0, 1), (3, 2))
+                for b in range(NH)
+            ],
+            axis=0,
         )
         value = jnp.dot(rows, down_v[...], preferred_element_type=F32).astype(BF)
-        count, first_block = SIZES[q] // 16, STARTS[q] // 16
+        count, first_block = SIZES[q] // 8, STARTS[q] // 8
         value = value.reshape(count, 2, 2, 16, 512)
         for b in range(count):
             part[:, first_block + b] = value[b]
@@ -386,8 +387,8 @@
 
     def stage_h(q):
         w, offsets = CHUNKS[q]
-        first_block = STARTS[q] // 16
-        blocks = pl.ds(first_block, SIZES[q] // 16)
+        first_block = STARTS[q] // 8
+        blocks = pl.ds(first_block, SIZES[q] // 8)
         arrived(part_in.at[blocks], oc_s.at[q], oc_r.at[q], across_c)
         z_send[blocks] = (part[c, blocks].astype(F32) + part_in[blocks].astype(F32)).astype(BF)
         for b, o in enumerate(offsets):
@@ -404,7 +405,7 @@
                 if kind == w and o:
                     offsets.append(o)
                 elif kind == w:
-                    total = z_send[STARTS[q] // 16 + b].astype(F32)
+                    total = z_send[STARTS[q] // 8 + b].astype(F32)
         for o in offsets:
             arrived(
                 z_recv.at[w, slot(o)], oz_s.at[w, slot(o)], oz_r.at[w, slot(o)],
@@ -424,7 +425,9 @@
                 e_send[0, rank] = rows_out[0, 4 * rank : 4 * rank + 4]
         else:
             for rank in range(DP):
-                fin[rank] = rows_out[1, 4 * rank : 4 * rank + 4] + in_listed[rank, 4:]
+                stream = in_listed[rank, 8:].astype(F32)
+                stream = jnp.where(parity == 1, stream[4:], stream[:4])
+                fin[rank] = rows_out[1, 4 * rank : 4 * rank + 4] + stream
             for rank in range(DP):
                 anchor = jnp.int32(rank)
                 for i in range(MIG):
@@ -434,15 +437,15 @@
 
     steps = {
         "local": local, "route": route, "listed": listed, "x": start_x, "y": start_y,
-        "w": forward, "a": stage_a, "b": stage_b, "c": stage_c, "d": stage_d, "e": stage_e,
+        "r": ring, "a": stage_a, "c": stage_c, "d": stage_d, "e": stage_e,
         "f": stage_f, "g": stage_g, "h": stage_h, "l": start_l, "m": start_m,
     }
     for step in ORDER:
         name = step.rstrip("0123456789")
         steps[name](int(step[len(name) :] or 0))
 
-    all_left(c_local, c_s.at[0], c_r.at[0])
-    all_left(c_listed, c_s.at[1], c_r.at[1])
+    all_left(in_local, c_s.at[0], c_r.at[0])
+    all_left(in_listed, c_s.at[1], c_r.at[1])
     for copy in sent:
         copy.wait_send()
     for w in range(2):
@@ -466,23 +469,19 @@
     smem = pl.BlockSpec(memory_space=pltpu.SMEM)
     nq = len(CHUNKS)
     dma = pltpu.SemaphoreType.DMA
-    share = (256, 512)
     scratch = [
         pltpu.VMEM((512, 2048), BF),
-        pltpu.VMEM((512, 512), BF), pltpu.VMEM((512, 512), BF), pltpu.VMEM((512, 512), BF),
+        pltpu.VMEM((2, 512, 512), BF), pltpu.VMEM((512, 512), BF),
         pltpu.VMEM((128, HD), F32), pltpu.VMEM((128, HD), F32), pltpu.VMEM((32, HD), F32),
         pltpu.VMEM((144, HD), BF), pltpu.VMEM((NX, 144, HD), BF),
         pltpu.VMEM((NH - 1, 144, HD), BF), pltpu.VMEM((NH, 144, HD), BF),
-        pltpu.VMEM((DP, 4, HD), F32), pltpu.VMEM((DP, 8, HD), F32),
-        pltpu.VMEM((DP, 4, HD), F32), pltpu.VMEM((DP, 8, HD), F32),
+        pltpu.VMEM((KVH, 8, HD), F32), pltpu.VMEM((KVH, 16, HD), BF),
+        pltpu.VMEM((DP, 8, HD), F32), pltpu.VMEM((DP, 16, HD), BF),
         pltpu.VMEM((64, HD), F32), pltpu.VMEM((DP * 8, HD), F32),
-        pltpu.VMEM((2, NZ, 2, 2, 16, 512), BF),
-        pltpu.VMEM((NX,) + share, BF), pltpu.VMEM((NX,) + share, BF),
-    ]
-    scratch += [pltpu.VMEM(share, BF) for _ in range(8)]
-    scratch += [
-        pltpu.VMEM((NH, 256, 256), BF), pltpu.VMEM((NH - 1, 256, 256), BF),
-        pltpu.VMEM((NX, NH, 256, HD), BF),
+        pltpu.VMEM((2, NZ, 2, 2, 16, 1024), BF),
+        pltpu.VMEM((2, 512, 512), BF), pltpu.VMEM((512, 512), BF),
+        pltpu.VMEM((NH, 128, 512), BF), pltpu.VMEM((NH - 1, 128, 512), BF),
+        pltpu.VMEM((NX, NH, 128, 256), BF),
         pltpu.VMEM((2, 16, 2, 16, 512), BF), pltpu.VMEM((16, 2, 16, 512), BF),
         pltpu.VMEM((16, 2, 16, 512), BF), pltpu.VMEM((2, NZ, 2, 16, 512), BF),
         pltpu.VMEM((2, 2, 16, 512), BF), pltpu.VMEM((2, 16, 512), BF),
@@ -492,9 +491,10 @@
     scratch += [dma((4,))]
     scratch += [dma((3,)) for _ in range(4)]
     scratch += [dma((2,)), dma((2,)), dma((2,)), dma((2,))]
-    scratch += [dma((2,)), dma((2,)), dma((2, NZ)), dma((2, NZ)), dma((2, NZ)), dma((2, NZ))]
-    scratch += [dma((nq, 6)), dma((nq, 6)), dma((nq, 3)), dma((nq, 3)), dma((nq, 3)), dma((nq, 3))]
-    scratch += [dma((nq, 4)), dma((nq, 4)), dma((nq,)), dma((nq,)), dma((2, NZ)), dma((2, NZ))]
+    scratch += [dma((2,)), dma((2,))]
+    scratch += [dma((2,)), dma((2,)), dma((2, NZ)), dma((2, NZ)), dma((2, 4)), dma((2, 4))]
+    scratch += [dma((nq,)), dma((nq,)), dma((nq, 3)), dma((nq, 3)), dma((nq, 3)), dma((nq, 3))]
+    scratch += [dma((nq, 3)), dma((nq, 3)), dma((nq,)), dma((nq,)), dma((2, NZ)), dma((2, NZ))]
     scratch += [dma((2,)), dma((2,))]
     done = pl.pallas_call(
         kernel,

time: 97.8 us -> 99.7 us (1.019); the launches traced: 96.5 us -> 99.4 us
  Pallas kernels: 95.1 us -> 98 us
    pallas_call x1, Pallas kernels: 95.1 us -> 98 us  [on_device(): pl.pallas_call(kernel, out_shape=jax.ShapeDtypeStruct((2, DP * 4 * HD), B...]
where the time goes in v4:
time: 99.7 us; the launch traced here: 99.4 us
  Pallas kernels  98 us (98%)
  local copies, waits for them, and re-layouts  1.4 us (1%)
    pallas_call x1, Pallas kernels, on_device(): pl.pallas_call(kernel, out_shape=jax.ShapeDtypeStruct((2, DP * 4 * HD), B...  98 us

profile of v4, /device:TPU:1, one launch (start us, length us, event | category | flops | bytes accessed | tf_op | source)
XLA Modules:
  0.0 99.4 jit_solution(4398987335158496096)
XLA Ops:
  0.0 98.0 %shard_map.109 = bf16[2,8192]{1,0:T(2,128)(2,1)} custom-call(s32[3,1,3]{2,1,0:T(1,128)} %bitcast.15, s32[2,16]{1,0:T(2,128)} %bitcast.16, s32[2]{0:T(128)} %bitcast.17, bf16[2,8192]{1,0:T(2,128)(2,1)} %bitcast.11, bf16[2,8192]{1,0:T(2,128)(2,1)} %bitcast.12, bf16[2,2048]{1,0:T(2,128)(2,1)} %bitcast.14, bf16[64,128]{1,0:T(8,128)(2,1)} %bitcast.13, ...), custom_call_target="tpu_custom_call" | custom-call | tf_op jit(solution)/shard_map/pallas_call | solution.py:499
  98.0 1.4 %copy.13 = bf16[1,1,2,8192]{3,2,1,0:T(2,128)(2,1)} copy(bf16[1,1,2,8192]{3,2,1,0:T(2,128)(2,1)} %bitcast.10) | data formatting | bytes 65536

commit v5 on v3

--- a/solution.py
+++ b/solution.py
@@ -20,13 +20,14 @@
 SIZES = [16 * len(offsets) for _, offsets in CHUNKS]
 STARTS = [sum(SIZES[:q]) for q in range(len(CHUNKS))]
 ORDER = (
-    "local", "x0", "route", "y0", "w0", "w1", "a0", "listed", "b0", "w2", "a1", "x1", "a2", "w3",
-    "b1", "y1", "c0", "a3", "c1", "b2", "b3", "d0", "w4", "w5", "c2", "a4", "w6", "w7", "d1",
-    "a5", "c3", "b4", "a7", "d2", "b5", "e0", "c4", "a6", "d3", "e1", "c5", "e2", "b6", "f0",
-    "b7", "d4", "f1", "f2", "e3", "c6", "d5", "c7", "g2", "e4", "g0", "g1", "f3", "d6", "h2",
-    "e5", "f4", "h0", "g3", "h1", "d7", "e6", "h3", "g4", "f5", "e7", "f6", "h4", "g5", "f7",
-    "g6", "h5", "l0", "g7", "h6", "h7", "m0", "l1", "m1",
+    "local", "x0", "route0", "route1", "y0", "listed0", "listed1", "w0", "listed2", "w2", "a0",
+    "w1", "a2", "x1", "w3", "b0", "a1", "y1", "b1", "c0", "b2", "a3", "c1", "w4", "c2", "b3",
+    "w5", "d0", "a4", "w6", "a5", "c3", "d2", "a6", "w7", "d1", "b5", "b4", "b6", "e0", "d3",
+    "a7", "c5", "e2", "c4", "f0", "b7", "c6", "f2", "e1", "d5", "e3", "d4", "g2", "c7", "f1",
+    "f3", "e5", "g0", "h2", "e4", "d6", "d7", "g3", "f4", "f5", "e6", "g1", "h3", "e7", "g4",
+    "h0", "h1", "f6", "g5", "f7", "h4", "g6", "h5", "l0", "g7", "h6", "h7", "m0", "l1", "m1",
 )
+ROUTED = (pl.ds(0, 80), pl.ds(80, 64))
 DISTANCES = (10, 9, 11, 8, 6, 14, 2, 5, 7, 13, 15, 4, 12, 1, 3)
 EPSILON = 1e-05
 BF = jnp.bfloat16
@@ -36,8 +37,8 @@
 def kernel(
     mig, table, lengths, q_in, res_in, new_in, gain, pool, gate_w, up_w, down_w, out,
     pool_v, gate_v, up_v, down_v,
-    q_t, res_t, new_t, own, line, y_send, y_recv, c_local, c_listed, in_local, in_listed,
-    stream_local, tiles, x_all,
+    q_t, res_t, new_t, own, line_q, line_res, y_send, y_recv, c_local, c_listed, in_local, in_listed,
+    stream_local, routed_row, attended_row, bias_row, tiles, x_all,
     gate_p, up_p, m1g, m1u, m2g, m2u, s3g, s3u, m3g, m3u,
     h_send, h_recv, hid, part, part_in, z_send, z_recv, l_send, l_recv,
     rows_out, fin, e_send, e_recv,
@@ -146,11 +147,11 @@
         odd = jnp.where(top_half, turned(first), second_value)
         return even, odd
 
-    own[...] = jnp.concatenate([q_t[64:], res_t[64:], new_t[16:]], axis=0).astype(BF)
+    own[...] = jnp.concatenate([q_t[64:], new_t[16:], res_t[64:]], axis=0).astype(BF)
 
     def bias_of(place):
         lane = lax.broadcasted_iota(jnp.int32, (8, MAXP * 2 * PG), 1)
-        page, inner = lane // PG, lane % PG
+        page, inner = lane >> 4, lane & 15
         length = lengths[place]
         filled = jnp.zeros_like(lane)
         for p in range(MAXP):
@@ -158,18 +159,20 @@
             filled = jnp.where(page == table[place, p], held, filled)
         return jnp.where(inner < filled, 0.0, -1e30)
 
-    def attend(q_rows, res_rows, new_rows, hidden_bias):
+    def attend(q_rows, new_rows, hidden_bias, first):
+        count = q_rows.shape[0]
+        heads = range(first, first + count)
         factor = 1.0 / math.sqrt(HD)
-        new_keys = jnp.stack([new_rows[j : j + 1] for j in range(KVH)])
-        new_values = jnp.stack([new_rows[KVH + j : KVH + j + 1] for j in range(KVH)])
+        new_keys = jnp.stack([new_rows[j : j + 1] for j in heads])
+        new_values = jnp.stack([new_rows[KVH + j : KVH + j + 1] for j in heads])
         q_bf = q_rows.astype(BF)
         score = jnp.stack(
             [
                 lax.dot_general(
-                    q_bf[head], pool_v[:, head * HD : (head + 1) * HD],
+                    q_bf[j - first], pool_v[:, j * HD : (j + 1) * HD],
                     (((1,), (1,)), ((), ())), preferred_element_type=F32,
                 )
-                for head in range(KVH)
+                for j in heads
             ]
         )
         score = score * factor + hidden_bias[None]
@@ -183,79 +186,100 @@
         attended = jnp.stack(
             [
                 jnp.dot(
-                    weight[head], pool_v[:, (KVH + head) * HD : (KVH + head + 1) * HD],
+                    weight[j - first], pool_v[:, (KVH + j) * HD : (KVH + j + 1) * HD],
                     preferred_element_type=F32,
                 )
-                for head in range(KVH)
+                for j in heads
             ]
         )
-        stream = res_rows + attended + own_weight * new_values
+        return attended + own_weight * new_values
+
+    def normalise(res_rows, attended):
+        stream = res_rows + attended
         square = jnp.sum(jnp.sum(stream * stream, axis=0), axis=-1, keepdims=True)
         mean = jnp.sum(square, axis=0, keepdims=True) * (1.0 / (DP * 4 * HD))
         scale = lax.rsqrt(mean + EPSILON)
-        normed = stream * scale[None] * gain[...].astype(F32).reshape(KVH, 8, HD)
-        return normed, stream
+        return stream * scale[None] * gain[...].astype(F32).reshape(KVH, 8, HD), stream
+
+    lines = (line_q, line_res)
 
     def local(_):
         local_q = q_t[:64].reshape(KVH, 8, HD)
         local_res = res_t[:64].reshape(KVH, 8, HD)
         hidden_bias = bias_of(1 - slot_id)
         use(0)
-        normed, stream = attend(local_q, local_res, new_t[:16], hidden_bias)
+        normed, stream = normalise(local_res, attend(local_q, new_t[:16], hidden_bias, 0))
         stream_local[...] = stream.reshape(DP * 4, HD)
         for k in range(DP):
             c_local[k] = normed[k // 2, 4 * (k % 2) : 4 * (k % 2) + 4]
         pl.semaphore_wait(barrier, len(partners))
         exchange(c_local, in_local, c_s.at[0], c_r.at[0])
-        for o in range(1, NX):
-            send(
-                own, line.at[x], rx_s.at[o - 1], rx_r.at[o - 1],
-                (h * NX + lax.rem(x + o, NX), tp),
-            )
-        line[x] = own[...]
+        for i, rows in enumerate(ROUTED):
+            for o in range(1, NX):
+                place = lax.rem(x + o, NX)
+                send(
+                    own.at[rows], lines[i].at[x], rx_s.at[i, o - 1], rx_r.at[i, o - 1],
+                    (h * NX + place, tp),
+                )
+            lines[i][x] = own[rows]
 
     sources = [mig[i, 0, 1] for i in range(MIG)]
     targets = [mig[i, 0, 2] for i in range(MIG)]
 
-    def route(_):
+    def route(i):
+        span_of = ROUTED[i]
         for o in range(1, NX):
             place = lax.rem(x + NX - o, NX)
-            arrived(line.at[place], rx_s.at[o - 1], rx_r.at[o - 1], (h * NX + place, tp))
-        rows = [line[lax.rem(target, NX)].astype(F32) for target in targets]
+            arrived(
+                lines[i].at[place], rx_s.at[i, o - 1], rx_r.at[i, o - 1],
+                (h * NX + place, tp),
+            )
+        rows = [lines[i][lax.rem(target, NX)].astype(F32) for target in targets]
         here = [lax.div(target, NX) == h for target in targets]
 
         def wanted(rank):
             value = jnp.zeros_like(rows[0])
-            for i in range(MIG):
-                value = jnp.where(here[i] & (sources[i] == rank), rows[i], value)
+            for j in range(MIG):
+                value = jnp.where(here[j] & (sources[j] == rank), rows[j], value)
             return value.astype(BF)
 
         for o in range(1, NH):
             place = lax.rem(h + o, NH)
-            y_send[o - 1] = wanted(place * NX + x)
+            y_send[o - 1, span_of] = wanted(place * NX + x)
             send(
-                y_send.at[o - 1], y_recv.at[o - 1], ry_s.at[o - 1], ry_r.at[o - 1], at_h(place)
-            )
-        y_recv[NH - 1] = wanted(dp)
-
-    def listed(_):
+                y_send.at[o - 1, span_of], y_recv.at[o - 1, span_of],
+                ry_s.at[i, o - 1], ry_r.at[i, o - 1], at_h(place),
+            )
+        y_recv[NH - 1, span_of] = wanted(dp)
+
+    def routed(i):
+        span_of = ROUTED[i]
         for o in range(1, NH):
             arrived(
-                y_recv.at[o - 1], ry_s.at[o - 1], ry_r.at[o - 1], at_h(lax.rem(h + NH - o, NH))
-            )
-        routed = y_recv[NH - 1].astype(F32)
+                y_recv.at[o - 1, span_of], ry_s.at[i, o - 1], ry_r.at[i, o - 1],
+                at_h(lax.rem(h + NH - o, NH)),
+            )
+        row = y_recv[NH - 1, span_of].astype(F32)
         for o in range(NH - 1):
-            routed = routed + y_recv[o].astype(F32)
+            row = row + y_recv[o, span_of].astype(F32)
         serves = (sources[0] == dp) | (sources[1] == dp) | (sources[2] == dp)
-        row = jnp.where(serves, routed, own[...].astype(F32))
-        normed, stream = attend(
-            row[:64].reshape(KVH, 8, HD), row[64:128].reshape(KVH, 8, HD), row[128:],
-            bias_of(slot_id),
-        )
-        even, odd = pieces(normed, stream)
-        for k in range(DP):
-            c_listed[k] = (even, odd)[k % 2][k // 2]
-        exchange(c_listed, in_listed, c_s.at[1], c_r.at[1])
+        return jnp.where(serves, row, own[span_of].astype(F32))
+
+    def listed(part):
+        if part == 0:
+            routed_row[...] = routed(0)
+            bias_row[...] = bias_of(slot_id)
+        if part < 2:
+            q_rows = routed_row[32 * part : 32 * part + 32].reshape(4, 8, HD)
+            attended_row[4 * part : 4 * part + 4] = attend(
+                q_rows, routed_row[64:], bias_row[...], 4 * part
+            )
+        else:
+            normed, stream = normalise(routed(1).reshape(KVH, 8, HD), attended_row[...])
+            even, odd = pieces(normed, stream)
+            for k in range(DP):
+                c_listed[k] = (even, odd)[k % 2][k // 2]
+            exchange(c_listed, in_listed, c_s.at[1], c_r.at[1])
 
     def start_x(w):
         source, count = (in_local, 4) if w == 0 else (in_listed, 8)
@@ -450,8 +474,9 @@
         for k in range(DP):
             tiles[64 * w + 4 * k : 64 * w + 4 * k + 4] = e_recv[w, k]
     tiles[:64] = tiles[:64] + stream_local[...]
-    value = jnp.concatenate([tiles[pl.ds(j, 2, stride=64), :] for j in range(64)], axis=1)
-    out[...] = ordered(value).astype(BF)
+    stays, moved = tiles[:64], tiles[64:]
+    out[:64] = jnp.where(second, stays, moved)
+    out[64:] = jnp.where(second, moved, stays)
     for w in range(2):
         all_left(e_send.at[w], e_s.at[w], e_r.at[w])
 
@@ -471,11 +496,12 @@
         pltpu.VMEM((512, 2048), BF),
         pltpu.VMEM((512, 512), BF), pltpu.VMEM((512, 512), BF), pltpu.VMEM((512, 512), BF),
         pltpu.VMEM((128, HD), F32), pltpu.VMEM((128, HD), F32), pltpu.VMEM((32, HD), F32),
-        pltpu.VMEM((144, HD), BF), pltpu.VMEM((NX, 144, HD), BF),
+        pltpu.VMEM((144, HD), BF), pltpu.VMEM((NX, 80, HD), BF), pltpu.VMEM((NX, 64, HD), BF),
         pltpu.VMEM((NH - 1, 144, HD), BF), pltpu.VMEM((NH, 144, HD), BF),
         pltpu.VMEM((DP, 4, HD), F32), pltpu.VMEM((DP, 8, HD), F32),
         pltpu.VMEM((DP, 4, HD), F32), pltpu.VMEM((DP, 8, HD), F32),
-        pltpu.VMEM((64, HD), F32), pltpu.VMEM((DP * 8, HD), F32),
+        pltpu.VMEM((64, HD), F32), pltpu.VMEM((80, HD), F32), pltpu.VMEM((KVH, 8, HD), F32),
+        pltpu.VMEM((8, MAXP * 2 * PG), F32), pltpu.VMEM((DP * 8, HD), F32),
         pltpu.VMEM((2, NZ, 2, 2, 16, 512), BF),
         pltpu.VMEM((NX,) + share, BF), pltpu.VMEM((NX,) + share, BF),
     ]
@@ -490,7 +516,7 @@
         pltpu.VMEM((2, DP, 4, HD), F32), pltpu.VMEM((2, DP, 4, HD), F32),
     ]
     scratch += [dma((4,))]
-    scratch += [dma((3,)) for _ in range(4)]
+    scratch += [dma((2, 3)) for _ in range(4)]
     scratch += [dma((2,)), dma((2,)), dma((2,)), dma((2,))]
     scratch += [dma((2,)), dma((2,)), dma((2, NZ)), dma((2, NZ)), dma((2, NZ)), dma((2, NZ))]
     scratch += [dma((nq, 6)), dma((nq, 6)), dma((nq, 3)), dma((nq, 3)), dma((nq, 3)), dma((nq, 3))]
@@ -498,7 +524,7 @@
     scratch += [dma((2,)), dma((2,))]
     done = pl.pallas_call(
         kernel,
-        out_shape=jax.ShapeDtypeStruct((2, DP * 4 * HD), BF),
+        out_shape=jax.ShapeDtypeStruct((2 * DP * 4, HD), F32),
         in_specs=[smem, smem, smem, vmem, vmem, vmem, vmem, hbm, hbm, hbm, hbm],
         out_specs=vmem,
         scratch_shapes=scratch,
@@ -510,7 +536,7 @@
         queries[0, 0], residual[0, 0], new_entries[0, 0], norm_gain.reshape(DP * 4, HD),
         page_pool.reshape(pages * page_rows, entry), gate_weight, up_weight, down_weight,
     )
-    return done.reshape(1, 1, 2, DP * 4 * HD)
+    return done.reshape(1, 1, 2, DP * 4 * HD).astype(BF)
 
 
 def solution(mesh):

time: 97.8 us -> 96.5 us (0.987); the launches traced: 96.5 us -> 96.2 us
    unnamed x1 -> x0, local copies, waits for them, and re-layouts: 1.4 us -> none
where the time goes in v5:
time: 96.5 us; the launch traced here: 96.2 us
  Pallas kernels  94.7 us (98%)
    pallas_call x1, Pallas kernels, on_device(): pl.pallas_call(kernel, out_shape=jax.ShapeDtypeStruct((2 * DP * 4, HD), F...  94.7 us

profile of v5, /device:TPU:1, one launch (start us, length us, event | category | flops | bytes accessed | tf_op | source)
XLA Modules:
  0.0 96.2 jit_solution(9582171427898699216)
XLA Ops:
  0.0 94.7 %shard_map.109 = f32[128,128]{1,0:T(8,128)} custom-call(s32[3,1,3]{2,1,0:T(1,128)} %bitcast.13, s32[2,16]{1,0:T(2,128)} %bitcast.14, s32[2]{0:T(128)} %bitcast.15, bf16[2,8192]{1,0:T(2,128)(2,1)} %bitcast.9, bf16[2,8192]{1,0:T(2,128)(2,1)} %bitcast.10, bf16[2,2048]{1,0:T(2,128)(2,1)} %bitcast.12, bf16[64,128]{1,0:T(8,128)(2,1)} %bitcast.11, ...), custom_call_target="tpu_custom_call" | custom-call | tf_op jit(solution)/shard_map/pallas_call | solution.py:525
  94.8 0.8 convert_element_type.14
  95.6 0.6 convert_element_type.15

commit v6 on v5

--- a/solution.py
+++ b/solution.py
@@ -29,6 +29,7 @@
 )
 ROUTED = (pl.ds(0, 80), pl.ds(80, 64))
 DISTANCES = (10, 9, 11, 8, 6, 14, 2, 5, 7, 13, 15, 4, 12, 1, 3)
+LAG = 16
 EPSILON = 1e-05
 BF = jnp.bfloat16
 F32 = jnp.float32
@@ -461,13 +462,19 @@
         "w": forward, "a": stage_a, "b": stage_b, "c": stage_c, "d": stage_d, "e": stage_e,
         "f": stage_f, "g": stage_g, "h": stage_h, "l": start_l, "m": start_m,
     }
+    counts, left_behind = [], 0
     for step in ORDER:
         name = step.rstrip("0123456789")
         steps[name](int(step[len(name) :] or 0))
+        counts.append(len(sent))
+        if len(counts) > LAG:
+            while left_behind < counts[-LAG]:
+                sent[left_behind].wait_send()
+                left_behind += 1
 
     all_left(c_local, c_s.at[0], c_r.at[0])
     all_left(c_listed, c_s.at[1], c_r.at[1])
-    for copy in sent:
+    for copy in sent[left_behind:]:
         copy.wait_send()
     for w in range(2):
         exchanged(e_recv.at[w], e_s.at[w], e_r.at[w])
@@ -475,8 +482,8 @@
             tiles[64 * w + 4 * k : 64 * w + 4 * k + 4] = e_recv[w, k]
     tiles[:64] = tiles[:64] + stream_local[...]
     stays, moved = tiles[:64], tiles[64:]
-    out[:64] = jnp.where(second, stays, moved)
-    out[64:] = jnp.where(second, moved, stays)
+    out[:64] = jnp.where(second, stays, moved).astype(BF)
+    out[64:] = jnp.where(second, moved, stays).astype(BF)
     for w in range(2):
         all_left(e_send.at[w], e_s.at[w], e_r.at[w])
 
@@ -524,7 +531,7 @@
     scratch += [dma((2,)), dma((2,))]
     done = pl.pallas_call(
         kernel,
-        out_shape=jax.ShapeDtypeStruct((2 * DP * 4, HD), F32),
+        out_shape=jax.ShapeDtypeStruct((2 * DP * 4, HD), BF),
         in_specs=[smem, smem, smem, vmem, vmem, vmem, vmem, hbm, hbm, hbm, hbm],
         out_specs=vmem,
         scratch_shapes=scratch,
@@ -536,7 +543,7 @@
         queries[0, 0], residual[0, 0], new_entries[0, 0], norm_gain.reshape(DP * 4, HD),
         page_pool.reshape(pages * page_rows, entry), gate_weight, up_weight, down_weight,
     )
-    return done.reshape(1, 1, 2, DP * 4 * HD).astype(BF)
+    return done.reshape(1, 1, 2, DP * 4 * HD)
 
 
 def solution(mesh):

time: 96.5 us -> 96.4 us (level)
    reshape x0 -> x1, local copies, waits for them, and re-layouts: none -> 1.39 us  [on_device(): return done.reshape(1, 1, 2, DP * 4 * HD)]
where the time goes in v6:
time: 96.4 us; the launch traced here: 96.2 us
  Pallas kernels  94.8 us (98%)
  local copies, waits for them, and re-layouts  1.39 us (1%)
    pallas_call x1, Pallas kernels, on_device(): pl.pallas_call(kernel, out_shape=jax.ShapeDtypeStruct((2 * DP * 4, HD), B...  94.8 us

profile of v6, /device:TPU:1, one launch (start us, length us, event | category | flops | bytes accessed | tf_op | source)
XLA Modules:
  0.0 96.2 jit_solution(13738584225460351482)
XLA Ops:
  0.0 94.8 %shard_map.109 = bf16[128,128]{1,0:T(8,128)(2,1)} custom-call(s32[3,1,3]{2,1,0:T(1,128)} %bitcast.13, s32[2,16]{1,0:T(2,128)} %bitcast.14, s32[2]{0:T(128)} %bitcast.15, bf16[2,8192]{1,0:T(2,128)(2,1)} %bitcast.9, bf16[2,8192]{1,0:T(2,128)(2,1)} %bitcast.10, bf16[2,2048]{1,0:T(2,128)(2,1)} %bitcast.12, bf16[64,128]{1,0:T(8,128)(2,1)} %bitcast.11, ...), custom_call_target="tpu_custom_call" | custom-call | tf_op jit(solution)/shard_map/pallas_call | solution.py:532
  94.8 1.4 %reshape.11 = bf16[1,1,2,8192]{3,2,1,0:T(2,128)(2,1)} reshape(bf16[128,128]{1,0:T(8,128)(2,1)} %shard_map.109) | data formatting | bytes 65536 | tf_op jit(solution)/shard_map/reshape | solution.py:546

commit v7 on v6

--- a/solution.py
+++ b/solution.py
@@ -92,10 +92,10 @@
     loads = [
         pltpu.make_async_copy(src, dst, load_sem.at[i])
         for i, (src, dst) in enumerate(
-            ((pool, pool_v), (gate_w, gate_v), (up_w, up_v), (down_w, down_v))
+            ((pool.at[:, pl.ds(0, KVH * HD)], pool_v.at[:, pl.ds(0, KVH * HD)]), (pool.at[:, pl.ds(KVH * HD, KVH * HD)], pool_v.at[:, pl.ds(KVH * HD, KVH * HD)]), (gate_w, gate_v), (up_w, up_v), (down_w, down_v))
         )
     ]
-    for copy in loads:
+    for copy in loads[:2]:
         copy.start()
     waiting = set(range(len(loads)))
 
@@ -148,7 +148,6 @@
         odd = jnp.where(top_half, turned(first), second_value)
         return even, odd
 
-    own[...] = jnp.concatenate([q_t[64:], new_t[16:], res_t[64:]], axis=0).astype(BF)
 
     def bias_of(place):
         lane = lax.broadcasted_iota(jnp.int32, (8, MAXP * 2 * PG), 1)
@@ -184,6 +183,7 @@
         scale = 1.0 / (jnp.sum(exponent, axis=-1, keepdims=True) + own_exponent)
         weight = (exponent * scale).astype(BF)
         own_weight = (own_exponent * scale).astype(BF).astype(F32)
+        use(1)
         attended = jnp.stack(
             [
                 jnp.dot(
@@ -209,12 +209,15 @@
         local_res = res_t[:64].reshape(KVH, 8, HD)
         hidden_bias = bias_of(1 - slot_id)
         use(0)
+        for copy in loads[2:]:
+            copy.start()
         normed, stream = normalise(local_res, attend(local_q, new_t[:16], hidden_bias, 0))
         stream_local[...] = stream.reshape(DP * 4, HD)
         for k in range(DP):
             c_local[k] = normed[k // 2, 4 * (k % 2) : 4 * (k % 2) + 4]
         pl.semaphore_wait(barrier, len(partners))
         exchange(c_local, in_local, c_s.at[0], c_r.at[0])
+        own[...] = jnp.concatenate([q_t[64:], new_t[16:], res_t[64:]], axis=0).astype(BF)
         for i, rows in enumerate(ROUTED):
             for o in range(1, NX):
                 place = lax.rem(x + o, NX)
@@ -317,8 +320,8 @@
         w, offsets = CHUNKS[q]
         for o in offsets:
             arrived(x_all.at[w, z_at(o), other_c], xc_s.at[w, slot(o)], xc_r.at[w, slot(o)], across_c)
-        use(1)
         use(2)
+        use(3)
         rows = jnp.concatenate([x_all[w, z_at(o)].reshape(64, 512) for o in offsets], axis=0)
         part_rows = span(q)
         for weight, dst in ((gate_v, gate_p), (up_v, up_p)):
@@ -397,7 +400,7 @@
         t = span(q)
         arrived(hid.at[xo, pl.ds(0, 2), t], xg_s.at[q, 2], xg_r.at[q, 2], left)
         arrived(hid.at[xo, pl.ds(2, 2), t], xg_s.at[q, 3], xg_r.at[q, 3], right)
-        use(3)
+        use(4)
         rows = jnp.concatenate(
             [jnp.concatenate([hid[a, b, t] for b in range(NH)], axis=1) for a in range(NX)], axis=0
         )
@@ -522,7 +525,7 @@
         pltpu.VMEM((2, 64, HD), F32), pltpu.VMEM((DP, 4, HD), F32),
         pltpu.VMEM((2, DP, 4, HD), F32), pltpu.VMEM((2, DP, 4, HD), F32),
     ]
-    scratch += [dma((4,))]
+    scratch += [dma((5,))]
     scratch += [dma((2, 3)) for _ in range(4)]
     scratch += [dma((2,)), dma((2,)), dma((2,)), dma((2,))]
     scratch += [dma((2,)), dma((2,)), dma((2, NZ)), dma((2, NZ)), dma((2, NZ)), dma((2, NZ))]

time: 96.4 us -> 96.2 us (level)
  no operation moved by 1% of the time
where the time goes in v7:
time: 96.2 us; the launch traced here: 95.8 us
  Pallas kernels  94.5 us (98%)
  local copies, waits for them, and re-layouts  1.39 us (1%)
    pallas_call x1, Pallas kernels, on_device(): pl.pallas_call(kernel, out_shape=jax.ShapeDtypeStruct((2 * DP * 4, HD), B...  94.5 us

profile of v7, /device:TPU:1, one launch (start us, length us, event | category | flops | bytes accessed | tf_op | source)
XLA Modules:
  0.0 95.8 jit_solution(12972763834487732980)
XLA Ops:
  0.0 94.5 %shard_map.109 = bf16[128,128]{1,0:T(8,128)(2,1)} custom-call(s32[3,1,3]{2,1,0:T(1,128)} %bitcast.13, s32[2,16]{1,0:T(2,128)} %bitcast.14, s32[2]{0:T(128)} %bitcast.15, bf16[2,8192]{1,0:T(2,128)(2,1)} %bitcast.9, bf16[2,8192]{1,0:T(2,128)(2,1)} %bitcast.10, bf16[2,2048]{1,0:T(2,128)(2,1)} %bitcast.12, bf16[64,128]{1,0:T(8,128)(2,1)} %bitcast.11, ...), custom_call_target="tpu_custom_call" | custom-call | tf_op jit(solution)/shard_map/pallas_call | solution.py:535
  94.5 1.4 %reshape.11 = bf16[1,1,2,8192]{3,2,1,0:T(2,128)(2,1)} reshape(bf16[128,128]{1,0:T(8,128)(2,1)} %shard_map.109) | data formatting | bytes 65536 | tf_op jit(solution)/shard_map/reshape | solution.py:549
